TPU v7x, 32 devices: a whole 2x2x4 slice. The times are simulated.
32 devices in a mesh: vocab: 8 (over z, y), tok: 4 (over x, core).
Axes of the slice: x: 2, y: 2, z: 4, core: 2. Of those that a mesh axis runs over, the one named last changes fastest.
Arguments:
- teacher_hidden: bfloat16 [512, 8192], P(None, 'tok'), may hold values from -80 to 80
- teacher_head: bfloat16 [8192, 81920], P('tok', 'vocab'), may hold values from -0.0625 to 0.0625
- student_hidden: bfloat16 [512, 3584], replicated, may hold values from -80 to 80
- student_head: bfloat16 [3584, 81920], P(None, ('vocab', 'tok')), may hold values from -0.09375 to 0.09375
- grammar_bits: int32 [512, 5120], P('tok', 'vocab'), may hold values from 0 to 65535
- sampled_ids: int32 [512], replicated, may hold values from 0 to 81919
Outputs:
- distill_loss: float32 [], replicated
- head_grad: bfloat16 [3584, 81920], P(None, ('vocab', 'tok'))
- hidden_grad: float32 [512, 3584], P(('vocab', 'tok'))
All inputs are finite; a program needn't handle non-finite values.
Results may differ from a plain program's by a relative error of at most 0.0038.
Values may be sent and summed in bfloat16 or wider, within the bound.
A program may use at most 192 MiB of HBM per device.

v0:
```python
import jax
import jax.numpy as jnp
from jax import lax
from jax.sharding import PartitionSpec as P

sample_weight = 0.5


def merged(part, axis, combine):
    gathered = jax.tree.map(lambda a: lax.all_gather(a, axis), part)

    def take(source):
        return jax.tree.map(lambda a: lax.dynamic_index_in_dim(a, source, 0, False), gathered)

    return lax.fori_loop(
        1, lax.axis_size(axis), lambda source, state: combine(state, take(source)), take(0)
    )


def admitted(packed, sampled_ids, column_start):
    shifts = jnp.arange(16, dtype=jnp.int32)
    bit_values = jnp.right_shift(packed[:, :, None], shifts[None, None, :]) & 1
    unpacked = bit_values.reshape(packed.shape[0], packed.shape[1] * 16)
    columns = column_start + jnp.arange(unpacked.shape[1], dtype=jnp.int32)
    chosen = columns[None, :] == sampled_ids[:, None]
    return ((unpacked == 1) | chosen, chosen)


def masked_stats(logits, allowed):
    masked = jnp.where(allowed, logits, -1e30)
    local_max = jnp.max(masked, axis=1)
    local_sum = jnp.sum(jnp.where(allowed, jnp.exp(masked - local_max[:, None]), 0.0), axis=1)
    return (local_max, local_sum)


def combine_stats(earlier, later):
    top = jnp.maximum(earlier[0], later[0])
    return (top, earlier[1] * jnp.exp(earlier[0] - top) + later[1] * jnp.exp(later[0] - top))


def teacher_side(logits, allowed, chosen, top, total):
    shifted = logits - top[:, None]
    prob = jnp.where(allowed, jnp.exp(shifted) / total[:, None], 0.0).astype(jnp.bfloat16)
    log_prob = shifted - jnp.log(total)[:, None]
    partial_loss = jnp.sum(jnp.where(allowed, prob.astype(jnp.float32) * log_prob, 0.0))
    partial_loss = partial_loss - sample_weight * jnp.sum(jnp.where(chosen, log_prob, 0.0))
    return (prob, partial_loss)


def per_device(
    teacher_hidden, teacher_head, student_hidden, student_head, grammar_bits, sampled_ids
):
    token_groups = lax.axis_size("tok")
    token_index = lax.axis_index("tok")
    vocab_index = lax.axis_index("vocab")
    token_total = student_hidden.shape[0]
    token_rows = token_total // token_groups
    teacher_cols = teacher_head.shape[1]
    student_cols = student_head.shape[1]
    student_start = (vocab_index * token_groups + token_index) * student_cols
    student_logit = jnp.dot(student_hidden, student_head, preferred_element_type=jnp.float32)
    own_max = jnp.max(student_logit, axis=1)
    own_sum = jnp.sum(jnp.exp(student_logit - own_max[:, None]), axis=1)
    student_max, student_sum = merged((own_max, own_sum), ("vocab", "tok"), combine_stats)
    student_log = student_logit - student_max[:, None] - jnp.log(student_sum)[:, None]
    student_columns = student_start + jnp.arange(student_cols, dtype=jnp.int32)
    student_chosen = student_columns[None, :] == sampled_ids[:, None]
    row_block = teacher_hidden
    teacher_logit = lax.psum_scatter(
        jnp.dot(row_block, teacher_head, preferred_element_type=jnp.float32),
        "tok",
        scatter_dimension=0,
        tiled=True,
    )
    ids_here = lax.dynamic_slice_in_dim(sampled_ids, token_index * token_rows, token_rows, 0)
    allowed, chosen = admitted(grammar_bits, ids_here, vocab_index * teacher_cols)
    local_max, local_sum = masked_stats(teacher_logit, allowed)
    teacher_max, teacher_sum = merged((local_max, local_sum), "vocab", combine_stats)
    block_prob, teacher_part = teacher_side(
        teacher_logit, allowed, chosen, teacher_max, teacher_sum
    )
    teacher_prob = lax.all_to_all(block_prob, "tok", split_axis=1, concat_axis=0, tiled=True)
    prob_wide = teacher_prob.astype(jnp.float32)
    student_part = -jnp.sum(prob_wide * student_log)
    student_part = student_part + sample_weight * jnp.sum(
        jnp.where(student_chosen, student_log, 0.0)
    )
    distill_loss = lax.psum(teacher_part + student_part, ("vocab", "tok")) / token_total
    logit_grad = (
        (1.0 - sample_weight) * jnp.exp(student_log)
        - prob_wide
        + sample_weight * student_chosen.astype(jnp.float32)
    ).astype(jnp.bfloat16)
    head_grad = lax.dot_general(
        student_hidden, logit_grad, (((0,), (0,)), ((), ())), preferred_element_type=jnp.float32
    ).astype(jnp.bfloat16)
    row_block = logit_grad
    hidden_grad = lax.psum_scatter(
        lax.dot_general(
            row_block, student_head, (((1,), (1,)), ((), ())), preferred_element_type=jnp.float32
        ),
        ("vocab", "tok"),
        scatter_dimension=0,
        tiled=True,
    )
    return (distill_loss, head_grad, hidden_grad)


def solution(mesh):
    placed = (
        P(None, "tok"),
        P("tok", "vocab"),
        P(),
        P(None, ("vocab", "tok")),
        P("tok", "vocab"),
        P(),
    )
    return jax.shard_map(
        per_device,
        mesh=mesh,
        in_specs=placed,
        out_specs=(P(), P(None, ("vocab", "tok")), P(("vocab", "tok"), None)),
        check_vma=False,
    )
```

profile of v0, /device:TPU:0, one launch (start us, length us, event | category | flops | bytes accessed | tf_op | source)
XLA Modules:
  0.0 459.8 jit_solution(1354248179285232887)
XLA Ops:
  7.2 0.0 copy-start
  7.2 0.0 reduce-scatter.3.cloned.1.call-start
  7.2 1.5 copy-done
  8.8 31.2 %fusion.10 = f32[512,10240]{1,0:T(8,128)} fusion(bf16[512,2048]{1,0:T(8,128)(2,1)S(1)} %copy-done, bf16[2048,10240]{1,0:T(8,128)(2,1)} %param.11), kind=kOutput, calls=%fused_computation.38 | convolution fusion | flops 21474836480 | bytes 65011712 | tf_op jit(solution)/shard_map/dot_general | solution.py:70
  39.9 0.0 reduce-scatter.3.cloned.1.call-update
  40.0 14.7 %fusion.9 = (f32[512]{0:T(512)S(1)}, f32[512,2560]{1,0:T(8,128)S(1)}) fusion(bf16[512,3584]{1,0:T(8,128)(2,1)} %param.12, bf16[3584,2560]{1,0:T(8,128)(2,1)} %param.13), kind=kOutput, calls=%fused_computation.37 | convolution fusion | flops 9396551680 | bytes 27265024 | tf_op jit(solution)/shard_map/dot_general | solution.py:61
  54.7 0.0 copy-start.3
  54.7 0.0 copy-start.5
  54.7 3.1 copy-done.3
  57.8 0.8 exponential_reduce_fusion
  58.7 43.9 %all-gather.7 = f32[32,1,512]{2,1,0:T(1,128)S(1)} all-gather(f32[1,1,512]{2,1,0:T(1,128)S(1)} %bitcast.74), channel_id=5, replica_groups=mesh['vocab'=8,'tok'=4] {'vocab','tok'}, dimensions={0}, use_global_device_ids=true | all-gather | bytes 67584 | tf_op jit(solution)/shard_map/all_gather | solution.py:10
  102.6 0.0 copy-start.6
  102.6 37.7 %all-gather.6 = f32[32,1,512]{2,1,0:T(1,128)S(1)} all-gather(f32[1,1,512]{2,1,0:T(1,128)S(1)} %bitcast.73), channel_id=4, replica_groups=mesh['vocab'=8,'tok'=4] {'vocab','tok'}, dimensions={0}, use_global_device_ids=true | all-gather | bytes 67584 | tf_op jit(solution)/shard_map/all_gather | solution.py:10
  140.3 0.0 copy-start.7
  140.3 0.0 copy-done.5
  140.3 0.2 copy.15
  140.5 0.1 shift_right_arithmetic.23
  140.7 2.7 shift_right_arithmetic.20
  143.4 0.0 copy-start.8
  143.4 5.9 %copy.16 = s32[128,10240]{1,0:T(8,128)} copy(s32[128,10240]{0,1:T(8,128)} %bitcast.62) | data formatting | bytes 10485760 | tf_op jit(solution)/shard_map/shift_right_arithmetic | solution.py:22
  149.3 0.0 copy-done.6
  149.3 0.0 copy-done.7
  149.3 0.0 copy-done.8
  149.3 0.1 dynamic_slice.57
  149.4 47.5 %reduce-scatter.3.cloned.1.call-done = f32[128,10240]{1,0:T(8,128)} async-done(((f32[512,10240]{1,0:T(8,128)}), f32[128,10240]{1,0:T(8,128)}) %reduce-scatter.3.cloned.1.call-update) | async-done | bytes 5242896 | tf_op jit(solution)/shard_map/reduce_scatter | solution.py:69
  196.8 0.0 copy-start.2
  196.8 5.4 %fusion.8 = (f32[128]{0:T(128)S(1)}, pred[128,10240]{1,0:T(8,128)(4,1)S(1)}) fusion(f32[128,10240]{1,0:T(8,128)} %reduce-scatter.3.cloned.1.call-done, s32[128]{0:T(128)S(1)} %dynamic_slice.57, s32[10240]{0:T(1024)S(1)} %iota_add_fusion, s32[128,10240]{1,0:T(8,128)} %copy.16, s32[10240]{0:T(1024)S(1)} %shift_right_arithmetic.23), kind=kLoop, calls=%fused_computation.30 | loop fusion | flops 9174912 | bytes 11879424 | tf_op jit(solution)/shard_map/reduce_max | solution.py:31
  202.3 0.1 copy-done.2
  202.4 1.5 select_reduce_fusion.1
  203.9 20.4 %all-gather.5 = f32[8,1,128]{2,1,0:T(1,128)S(1)} all-gather(f32[1,1,128]{2,1,0:T(1,128)S(1)} %bitcast.76), channel_id=3, replica_groups=mesh['vocab'=8,'tok'=4] {'vocab'}, dimensions={0}, use_global_device_ids=true | all-gather | bytes 4608 | tf_op jit(solution)/shard_map/all_gather | solution.py:10
  224.3 16.1 %all-gather.4 = f32[8,1,128]{2,1,0:T(1,128)S(1)} all-gather(f32[1,1,128]{2,1,0:T(1,128)S(1)} %bitcast.75), channel_id=2, replica_groups=mesh['vocab'=8,'tok'=4] {'vocab'}, dimensions={0}, use_global_device_ids=true | all-gather | bytes 4608 | tf_op jit(solution)/shard_map/all_gather | solution.py:10
  240.4 0.3 while.34
  240.7 5.1 %fusion.3 = (f32[]{:T(128)}, f32[]{:T(128)}, bf16[128,10240]{1,0:T(8,128)(2,1)S(1)}) fusion(f32[128,10240]{1,0:T(8,128)} %reduce-scatter.3.cloned.1.call-done, f32[128]{0:T(128)S(1)} %log.6, f32[128]{0:T(128)S(1)} %get-tuple-element.269, s32[10240]{0:T(1024)S(1)} %iota_add_fusion, s32[128]{0:T(128)S(1)} %dynamic_slice.57, ...), kind=kLoop, calls=%fused_computation.15 | loop fusion | flops 15728638 | bytes 9218056 | tf_op jit(solution)/shard_map/reduce_sum | solution.py:46
  245.8 0.0 slice-start
  245.8 0.0 slice-start.1
  245.8 1.7 copy.25
  247.5 4.5 all-to-all-start
  252.1 0.0 reduce-scatter.5.cloned.1.call-start
  252.1 0.0 slice-done
  252.1 0.0 slice-done.1
  252.1 1.8 while.35
  254.0 29.5 %all-to-all-done = bf16[128,4,2560]{2,0,1:T(8,128)(2,1)} async-done(((bf16[128,4,2560]{2,0,1:T(8,128)(2,1)}), bf16[128,4,2560]{2,0,1:T(8,128)(2,1)}, u32[]{:S(2)}, u32[]{:S(2)}) %all-to-all-start) | async-done | bytes 2621472 | tf_op jit(solution)/shard_map/all_to_all | solution.py:82
  283.4 6.9 %fusion.4 = (f32[]{:T(128)}, f32[]{:T(128)}, bf16[512,2560]{1,0:T(8,128)(2,1)S(1)}) fusion(f32[512,2560]{1,0:T(8,128)} %copy-done.3, s32[2560]{0:T(1024)S(1)} %iota_add_fusion.1, f32[512]{0:T(512)S(1)} %log.7, f32[512]{0:T(512)S(1)} %get-tuple-element.271, s32[512]{0:T(512)S(1)} %copy-done.8, bf16[128,4,2560]{2,0,1:T(8,128)(2,1)} %all-to-all-done), kind=kLoop, calls=%fused_computation.16 | loop fusion | flops 17039358 | bytes 10502152 | tf_op jit(solution)/shard_map/reduce_sum | solution.py:85
  290.3 0.0 copy-start.4
  290.3 1.5 copy-done.4
  291.8 15.4 %fusion.11 = f32[512,3584]{1,0:T(8,128)} fusion(bf16[512,2560]{1,0:T(8,128)(2,1)S(1)} %get-tuple-element.315, bf16[3584,2560]{1,0:T(8,128)(2,1)} %param.13), kind=kOutput, calls=%fused_computation.39 | convolution fusion | flops 9395240960 | bytes 28311552 | tf_op jit(solution)/shard_map/dot_general | solution.py:99
  307.2 0.0 reduce-scatter.5.cloned.1.call-update
  309.9 39.8 %psum.7 = f32[]{:T(128)} all-reduce(f32[]{:T(128)S(6)} %add.142), channel_id=1, replica_groups=mesh['vocab'=8,'tok'=4] {'vocab','tok'}, use_global_device_ids=true, to_apply=%region_13.14 | all-reduce | flops 1 | bytes 8 | tf_op jit(solution)/shard_map/psum | solution.py:88
  349.6 15.8 %fusion.2 = bf16[3584,2560]{0,1:T(8,128)(2,1)} fusion(bf16[512,2560]{1,0:T(8,128)(2,1)} %copy-done.4, bf16[512,3584]{1,0:T(8,128)(2,1)} %param.12), kind=kOutput, calls=%fused_computation.10 | convolution fusion | flops 9404416000 | bytes 24641536 | tf_op jit(solution)/shard_map/dot_general | solution.py:94
  365.5 0.0 copy-start.1
  365.5 25.3 %copy.18 = bf16[3584,2560]{1,0:T(8,128)(2,1)} copy(bf16[3584,2560]{0,1:T(8,128)(2,1)} %fusion.2) | data formatting | bytes 36700160
  391.4 60.5 %reduce-scatter.5.cloned.1.call-done = f32[16,3584]{1,0:T(8,128)} async-done(((f32[512,3584]{1,0:T(8,128)}), f32[16,3584]{1,0:T(8,128)}) %reduce-scatter.5.cloned.1.call-update) | async-done | bytes 229392 | tf_op jit(solution)/shard_map/reduce_scatter | solution.py:98
  451.9 0.0 copy-done.1
  (78 shorter events, 1.3 us)
Async XLA Ops:
  7.2 1.6 copy-start
  7.2 189.7 %reduce-scatter.3.cloned.1.call-start = ((), (), s32[]{:S(2)}) async-start(), calls=%async_computation.3 | async-start | bytes 26214400 | tf_op jit(solution)/shard_map/reduce_scatter | solution.py:69
  54.7 3.2 copy-start.3
  54.7 85.6 %copy-start.5 = (s32[128,640]{1,0:T(8,128)S(1)}, s32[128,640]{1,0:T(8,128)}, u32[]{:S(2)}) copy-start(s32[128,640]{1,0:T(8,128)} %param.14) | copy-start | bytes 983044
  102.6 46.7 %copy-start.6 = (f32[32,1,512]{2,1,0:T(1,128)}, f32[32,1,512]{2,1,0:T(1,128)S(1)}, u32[]{:S(2)}) copy-start(f32[32,1,512]{2,1,0:T(1,128)S(1)} %all-gather.7) | copy-start | bytes 196612
  140.3 9.0 %copy-start.7 = (f32[32,1,512]{2,1,0:T(1,128)}, f32[32,1,512]{2,1,0:T(1,128)S(1)}, u32[]{:S(2)}) copy-start(f32[32,1,512]{2,1,0:T(1,128)S(1)} %all-gather.6) | copy-start | bytes 196612
  143.4 5.9 %copy-start.8 = (s32[512]{0:T(512)S(1)}, s32[512]{0:T(512)}, u32[]{:S(2)}) copy-start(s32[512]{0:T(512)} %param.15) | copy-start | bytes 6148
  196.8 5.5 %copy-start.2 = (f32[128,10240]{1,0:T(8,128)S(1)}, f32[128,10240]{1,0:T(8,128)}, u32[]{:S(2)}) copy-start(f32[128,10240]{1,0:T(8,128)} %reduce-scatter.3.cloned.1.call-done) | copy-start | bytes 15728644
  245.8 6.3 %slice-start = ((f32[32,1,512]{2,1,0:T(1,128)}), f32[1,1,512]{2,1,0:T(1,128)S(1)}, s32[]{:S(2)}) async-start(f32[32,1,512]{2,1,0:T(1,128)} %copy-done.6), calls=%async_computation.5 | async-start | bytes 4096 | tf_op jit(solution)/shard_map/jit(dynamic_index_in_dim)/dynamic_slice | solution.py:13
  245.8 6.3 %slice-start.1 = ((f32[32,1,512]{2,1,0:T(1,128)}), f32[1,1,512]{2,1,0:T(1,128)S(1)}, s32[]{:S(2)}) async-start(f32[32,1,512]{2,1,0:T(1,128)} %copy-done.7), calls=%async_computation.6 | async-start | bytes 4096 | tf_op jit(solution)/shard_map/jit(dynamic_index_in_dim)/dynamic_slice | solution.py:13
  247.5 35.9 %all-to-all-start = ((bf16[128,4,2560]{2,0,1:T(8,128)(2,1)}), bf16[128,4,2560]{2,0,1:T(8,128)(2,1)}, u32[]{:S(2)}, u32[]{:S(2)}) async-start(bf16[128,4,2560]{2,0,1:T(8,128)(2,1)} %bitcast.63), calls=%async_computation.1 | async-start | bytes 5242880 | tf_op jit(solution)/shard_map/all_to_all | solution.py:82
  252.1 199.8 %reduce-scatter.5.cloned.1.call-start = ((), (), s32[]{:S(2)}) async-start(), calls=%async_computation.4 | async-start | bytes 7569408 | tf_op jit(solution)/shard_map/reduce_scatter | solution.py:98
  290.3 1.5 copy-start.4
  365.5 86.4 %copy-start.1 = (bf16[512,2048]{1,0:T(8,128)(2,1)S(1)}, bf16[512,2048]{1,0:T(8,128)(2,1)}, u32[]{:S(2)}) copy-start(bf16[512,2048]{1,0:T(8,128)(2,1)} %param.10) | copy-start | bytes 6291460
Sparse Core Ops, SparseCore 0:
  40.1 156.7 reduce-scatter.2
  307.3 144.4 reduce-scatter.4
where the time goes:
time: 461 us; the launch traced here: 460 us
  blocking collectives  158 us (34%)
  waiting for transfers between devices  137 us (30%)
  matrix products  77.1 us (17%)
  local copies, waits for them, and re-layouts  42.7 us (9%)
  other arithmetic  20.6 us (4%)
  between operations  18.6 us (4%)
  starting transfers between devices  4.62 us (1%)
    all_gather x4, blocking collectives, merged(): gathered = jax.tree.map(lambda a: lax.all_gather(a, axis), part)  118 us
    reduce_scatter x1, waiting for transfers between devices, per_device(): lax.psum_scatter(lax.dot_general(row_block, student_head, (((1,), (1,)),...  60.5 us
    reduce_scatter x1, waiting for transfers between devices, per_device(): lax.psum_scatter(jnp.dot(row_block, teacher_head, preferred_element_type=...  47.5 us
    psum x1, blocking collectives, per_device(): lax.psum(teacher_part + student_part, ('vocab', 'tok')) / token_total  39.8 us
    unnamed x22, local copies, waits for them, and re-layouts  31.8 us
    dot_general x1, matrix products, per_device(): jnp.dot(row_block, teacher_head, preferred_element_type=jnp.float32)  31.2 us
    all_to_all x1, waiting for transfers between devices, per_device(): lax.all_to_all(block_prob, 'tok', split_axis=1, concat_axis=0, tiled=True)  29.5 us
    dot_general x1, matrix products, per_device(): lax.dot_general(student_hidden, logit_grad, (((0,), (0,)), ((), ())), pre...  15.8 us
  transfers between devices with their start and end apart: 3, of which 3 were waited for; matrix products, arithmetic and copies ran while one was open for 15% of the time, Pallas kernels for 0%

commit v1 on v0

v1 whole, which is shorter than its diff:
```python
import functools

import jax
import jax.numpy as jnp
from jax import lax
from jax.experimental import pallas as pl
from jax.experimental.pallas import tpu as pltpu
from jax.sharding import PartitionSpec as P

sample_weight = 0.5
grad_scale = 4096.0
MESH = pl.DeviceIdType.MESH


def bits_of(size):
    return size.bit_length() - 1


def swapped(value, axis, bit):
    size = lax.axis_size(axis)
    return lax.ppermute(value, axis, [(i, i ^ (1 << bit)) for i in range(size)])


def chunk_kernel(first_ref, a_ref, b_ref, *rest):
    out_ref = rest[-1]
    total = jnp.dot(a_ref[...], b_ref[...], preferred_element_type=jnp.float32)
    for extra in rest[:-1]:
        total = total + extra[...].astype(jnp.float32)
    out_ref[...] = total.astype(out_ref.dtype)


def chunk_product(a, b, first, width, tile, out_dtype, extras=()):
    rows, depth = a.shape
    tiles = width // tile
    grid_spec = pltpu.PrefetchScalarGridSpec(
        num_scalar_prefetch=1,
        grid=(tiles,),
        in_specs=[
            pl.BlockSpec((rows, depth), lambda i, f: (0, 0)),
            pl.BlockSpec((depth, tile), lambda i, f: (0, f[0] + i)),
        ]
        + [pl.BlockSpec((rows, tile), lambda i, f: (0, i)) for _ in extras],
        out_specs=pl.BlockSpec((rows, tile), lambda i, f: (0, i)),
    )
    return pl.pallas_call(
        chunk_kernel,
        grid_spec=grid_spec,
        out_shape=jax.ShapeDtypeStruct((rows, width), out_dtype),
        compiler_params=pltpu.CompilerParams(vmem_limit_bytes=40 * 1024 * 1024),
        cost_estimate=pl.CostEstimate(
            flops=2 * rows * depth * width,
            bytes_accessed=2 * (rows * depth + depth * width + 2 * rows * width),
            transcendentals=0,
        ),
    )((first // tile).reshape(1).astype(jnp.int32), a, b, *extras)


def grad_kernel(hidden_ref, grad_ref, *rest):
    rest[-1][...] = lax.dot_general(
        hidden_ref[...],
        grad_ref[...],
        (((0,), (0,)), ((), ())),
        preferred_element_type=jnp.float32,
    ).astype(jnp.bfloat16)


def grad_rows(hidden, grad, earlier, step, tile):
    tokens, width = hidden.shape
    columns = grad.shape[1]
    cut = 2 if columns % 256 == 0 else 1
    held = () if earlier is None else (earlier,)
    return pl.pallas_call(
        grad_kernel,
        grid=(cut,),
        in_specs=[
            pl.BlockSpec((tokens, tile), lambda i: (0, step)),
            pl.BlockSpec((tokens, columns // cut), lambda i: (0, i)),
        ]
        + [pl.BlockSpec(memory_space=pl.ANY) for _ in held],
        out_specs=pl.BlockSpec((tile, columns // cut), lambda i: (step, i)),
        out_shape=jax.ShapeDtypeStruct((width, columns), jnp.bfloat16),
        input_output_aliases={2: 0} if held else {},
        compiler_params=pltpu.CompilerParams(vmem_limit_bytes=24 * 1024 * 1024),
        cost_estimate=pl.CostEstimate(
            flops=2 * tokens * tile * columns,
            bytes_accessed=2 * (tokens * tile + tokens * columns + tile * columns),
            transcendentals=0,
        ),
    )(hidden, grad, *held)


def merge_rows(parts):
    teacher_top = jnp.max(parts[:, 0, :], axis=0, keepdims=True)
    student_top = jnp.max(parts[:, 3, :], axis=0, keepdims=True)
    teacher_shift = parts[:, 0, :] - teacher_top
    student_shift = parts[:, 3, :] - student_top
    scale = jnp.exp(teacher_shift)
    teacher_sum = jnp.sum(parts[:, 1, :] * scale, axis=0, keepdims=True)
    cross = jnp.sum(
        scale * (parts[:, 2, :] + parts[:, 1, :] * (teacher_shift - student_shift)),
        axis=0,
        keepdims=True,
    )
    student_sum = jnp.sum(parts[:, 4, :] * jnp.exp(student_shift), axis=0, keepdims=True)
    picked = jnp.sum(parts[:, 5, :], axis=0, keepdims=True)
    return jnp.concatenate(
        [teacher_top, teacher_sum, cross, student_top, student_sum, picked, picked, picked], axis=0
    )


def stats_kernel(
    groups, ways, part_ref, out_ref, tok_ref, vocab_ref, send_a, recv_a, send_b, recv_b
):
    mine = lax.axis_index("tok")
    place = lax.axis_index("vocab")
    barrier = pltpu.get_barrier_semaphore()
    for step in range(1, groups):
        pl.semaphore_signal(
            barrier,
            inc=1,
            device_id=(place, lax.rem(mine + step, groups)),
            device_id_type=MESH,
        )
    for step in range(1, ways):
        pl.semaphore_signal(
            barrier,
            inc=1,
            device_id=(lax.rem(place + step, ways), mine),
            device_id_type=MESH,
        )
    pl.semaphore_wait(barrier, groups + ways - 2)
    tok_ref[0] = part_ref[...]
    copies = []
    for step in range(1, groups):
        copy = pltpu.make_async_remote_copy(
            src_ref=part_ref,
            dst_ref=tok_ref.at[step],
            send_sem=send_a.at[step],
            recv_sem=recv_a.at[step],
            device_id=(place, lax.rem(mine + step, groups)),
            device_id_type=MESH,
        )
        copy.start()
        copies.append(copy)
    for copy in copies:
        copy.wait()
    vocab_ref[0] = merge_rows(tok_ref[...])
    copies = []
    for step in range(1, ways):
        copy = pltpu.make_async_remote_copy(
            src_ref=vocab_ref.at[0],
            dst_ref=vocab_ref.at[step],
            send_sem=send_b.at[step],
            recv_sem=recv_b.at[step],
            device_id=(lax.rem(place + step, ways), mine),
            device_id_type=MESH,
        )
        copy.start()
        copies.append(copy)
    for copy in copies:
        copy.wait()
    out_ref[...] = merge_rows(vocab_ref[...])


def merged_stats(part):
    groups = lax.axis_size("tok")
    ways = lax.axis_size("vocab")
    return pl.pallas_call(
        functools.partial(stats_kernel, groups, ways),
        out_shape=jax.ShapeDtypeStruct(part.shape, jnp.float32),
        in_specs=[pl.BlockSpec(memory_space=pltpu.VMEM)],
        out_specs=pl.BlockSpec(memory_space=pltpu.VMEM),
        scratch_shapes=[
            pltpu.VMEM((groups,) + part.shape, jnp.float32),
            pltpu.VMEM((ways,) + part.shape, jnp.float32),
            pltpu.SemaphoreType.DMA((groups,)),
            pltpu.SemaphoreType.DMA((groups,)),
            pltpu.SemaphoreType.DMA((ways,)),
            pltpu.SemaphoreType.DMA((ways,)),
        ],
        compiler_params=pltpu.CompilerParams(collective_id=0, has_side_effects=True),
    )(part)


def words_here(grammar_bits, width):
    groups = lax.axis_size("tok")
    mine = lax.axis_index("tok")
    pieces = grammar_bits.reshape(grammar_bits.shape[0], groups, width)
    got = [lax.dynamic_index_in_dim(pieces, mine, 1, False)]
    for step in range(1, groups):
        piece = lax.dynamic_index_in_dim(pieces, mine ^ step, 1, False)
        got.append(lax.ppermute(piece, "tok", [(i, i ^ step) for i in range(groups)]))
    stacked = jnp.stack(got)
    return jnp.concatenate(
        [lax.dynamic_index_in_dim(stacked, mine ^ block, 0, False) for block in range(groups)]
    )


def admitted(words, columns):
    width = words.shape[1]
    low = (words & 255).astype(jnp.bfloat16)
    high = jnp.right_shift(words, 8).astype(jnp.bfloat16)
    spread = jnp.arange(columns, dtype=jnp.int32)
    sources = jnp.arange(2 * width, dtype=jnp.int32)
    wanted = spread // 16 + jnp.where(spread % 16 >= 8, width, 0)
    picks = (sources[:, None] == wanted[None, :]).astype(jnp.bfloat16)
    octets = jnp.dot(
        jnp.concatenate([low, high], axis=1), picks, preferred_element_type=jnp.float32
    ).astype(jnp.int32)
    return jnp.right_shift(octets, (spread % 8)[None, :]) & 1


def split_rows(value):
    groups, ways = lax.axis_size("tok"), lax.axis_size("vocab")
    left = [("vocab", b) for b in reversed(range(bits_of(ways)))]
    left += [("tok", b) for b in reversed(range(bits_of(groups)))]
    rows = value.shape[0] // (groups * ways)
    return left, value.reshape((2,) * len(left) + (rows, value.shape[1]))


def halves_of(total, left, key):
    at = left.index(key)
    bit = (lax.axis_index(key[0]) >> key[1]) & 1
    away = lax.dynamic_index_in_dim(total, 1 - bit, at, False).astype(jnp.float16)
    return away, lax.dynamic_index_in_dim(total, bit, at, False).astype(jnp.float32)


def per_device(
    teacher_hidden, teacher_head, student_hidden, student_head, grammar_bits, sampled_ids
):
    groups = lax.axis_size("tok")
    mine = lax.axis_index("tok")
    place = lax.axis_index("vocab")
    token_total = student_hidden.shape[0]
    columns = student_head.shape[1]
    start = (place * groups + mine) * columns
    tile = 256
    half = columns // 2

    def product(target, lower, dtype, extras=()):
        return chunk_product(
            teacher_hidden, teacher_head, target * columns + lower, half, tile, dtype, extras
        )

    far, near = [], []
    for lower in (0, half):
        away = product(mine ^ 3, lower, jnp.float32)
        far.append(swapped(away, "tok", 0))
    sent = []
    for at, lower in enumerate((0, half)):
        away = product(mine ^ 2, lower, jnp.float32, (far[at],))
        sent.append(swapped(away.astype(jnp.float16), "tok", 1))
    for lower in (0, half):
        away = product(mine ^ 1, lower, jnp.float32)
        near.append(swapped(away, "tok", 0))
    own = [product(mine, lower, jnp.float32, (near[at],)) for at, lower in enumerate((0, half))]

    student_logit = jnp.dot(student_hidden, student_head, preferred_element_type=jnp.float32)
    student_top = jnp.max(student_logit, axis=1)
    student_sum = jnp.sum(jnp.exp(student_logit - student_top[:, None]), axis=1)
    bit = admitted(words_here(grammar_bits, columns // 16), columns)
    here = start + jnp.arange(columns, dtype=jnp.int32)
    chosen = here[None, :] == sampled_ids[:, None]
    penalty = jnp.where((bit == 1) | chosen, 0.0, -1e30).astype(jnp.bfloat16)

    teacher_logit = jnp.concatenate(
        [own[at] + sent[at].astype(jnp.float32) for at in range(2)], axis=1
    )
    masked = jnp.where(penalty < 0, -1e30, teacher_logit)
    top = jnp.max(masked, axis=1)
    shifted = masked - top[:, None]
    weight = jnp.where(penalty < 0, 0.0, jnp.exp(shifted))
    weight_sum = jnp.sum(weight, axis=1)
    cross = jnp.sum(
        jnp.where(
            penalty < 0, 0.0, weight * (shifted - (student_logit - student_top[:, None]))
        ),
        axis=1,
    )
    picked = jnp.sum(jnp.where(chosen, student_logit - masked, 0.0), axis=1)
    zero = jnp.zeros_like(top)
    part = jnp.stack([top, weight_sum, cross, student_top, student_sum, picked, zero, zero])
    merged = merged_stats(part)
    teacher_top, teacher_sum, cross, student_top, student_sum, picked = (
        merged[i] for i in range(6)
    )
    teacher_lse = jnp.log(teacher_sum)
    student_lse = jnp.log(student_sum)
    divergence = cross / teacher_sum - teacher_lse + student_lse
    gap = picked + (teacher_top - student_top) + (teacher_lse - student_lse)
    distill_loss = jnp.sum(divergence + sample_weight * gap) / token_total

    prob = jnp.where(
        penalty < 0, 0.0, jnp.exp(masked - teacher_top[:, None]) / teacher_sum[:, None]
    ).astype(jnp.bfloat16)
    student_log = student_logit - student_top[:, None] - student_lse[:, None]
    logit_grad = (
        (1.0 - sample_weight) * jnp.exp(student_log)
        - prob.astype(jnp.float32)
        + sample_weight * chosen.astype(jnp.float32)
    ).astype(jnp.bfloat16)

    tok_bits = [("tok", b) for b in range(bits_of(groups))]
    vocab_bits = [("vocab", b) for b in range(bits_of(lax.axis_size("vocab")))]
    orders = (
        tok_bits + vocab_bits,
        tok_bits[:1] + vocab_bits[:1] + tok_bits[1:] + vocab_bits[1:],
    )
    width = student_head.shape[0] // 2
    blocks = []
    for at in range(2):
        block = lax.dot_general(
            logit_grad,
            lax.slice_in_dim(student_head, at * width, (at + 1) * width, axis=0),
            (((1,), (1,)), ((), ())),
            preferred_element_type=jnp.float32,
        )
        blocks.append(block * grad_scale)
    step_rows = 512 if student_hidden.shape[1] % 512 == 0 else 128
    steps = student_hidden.shape[1] // step_rows
    levels = len(orders[0])
    shares = [2, 3, 1, 1] + [0] * levels
    head_grad = None
    step = 0
    lefts, totals = zip(*[split_rows(block) for block in blocks])
    for level in range(levels):
        aways, keeps = [], []
        for at in range(2):
            away, keep = halves_of(totals[at], lefts[at], orders[at][level])
            aways.append(away)
            keeps.append(keep)
        *aways, logit_grad = lax.optimization_barrier((*aways, logit_grad))
        got = [swapped(aways[at], *orders[at][level]) for at in range(2)]
        until = steps if level == levels - 1 else min(steps, step + shares[level])
        if until > step:
            while step < until:
                head_grad = grad_rows(student_hidden, logit_grad, head_grad, step, step_rows)
                step += 1
            *got, head_grad = lax.optimization_barrier((*got, head_grad))
        totals = [keeps[at] + got[at].astype(jnp.float32) for at in range(2)]
        for at in range(2):
            lefts[at].remove(orders[at][level])
    hidden_grad = jnp.concatenate(totals, axis=1) * (1.0 / grad_scale)
    return (distill_loss, head_grad, hidden_grad)


def solution(mesh):
    placed = (
        P(None, "tok"),
        P("tok", "vocab"),
        P(),
        P(None, ("vocab", "tok")),
        P("tok", "vocab"),
        P(),
    )
    return jax.shard_map(
        per_device,
        mesh=mesh,
        in_specs=placed,
        out_specs=(P(), P(None, ("vocab", "tok")), P(("vocab", "tok"), None)),
        check_vma=False,
    )
```

time: 461 us -> 229 us (0.50)
  blocking collectives: 158 us -> 0 us
  waiting for transfers between devices: 137 us -> 43 us
  Pallas kernels: 0 us -> 88.9 us
  matrix products: 77.1 us -> 36.7 us
  local copies, waits for them, and re-layouts: 42.7 us -> 15.1 us
  between operations: 18.6 us -> 2.93 us
  starting transfers between devices: 4.62 us -> 16.2 us
    all_gather x4 -> x0, blocking collectives: 118 us -> none  [merged(): gathered = jax.tree.map(lambda a: lax.all_gather(a, axis), part)]
    reduce_scatter x2 -> x0, waiting for transfers between devices: 108 us -> none  [the longest x1 60.5 us: per_device(): lax.psum_scatter(lax.dot_general(row_block, student_head, (((1,), (1,)),...]
    pallas_call x0 -> x16, Pallas kernels: none -> 88.9 us  [the longest x8 54.2 us: chunk_product(): pl.pallas_call(chunk_kernel, grid_spec=grid_spec, out_shape=jax.ShapeDtyp...]
    ppermute x0 -> x19, waiting for transfers between devices: none -> 43 us  [the longest x16 41.7 us: swapped(): return lax.ppermute(value, axis, [(i, i ^ 1 << bit) for i in range(size)])]
    dot_general x3, matrix products: 62.4 us -> 20.5 us  [the longest x2 16.3 us: per_device(): lax.dot_general(logit_grad, lax.slice_in_dim(student_head, at * width, (a...]
    psum x1 -> x0, blocking collectives: 39.8 us -> none  [per_device(): lax.psum(teacher_part + student_part, ('vocab', 'tok')) / token_total]
    all_to_all x1 -> x0, waiting for transfers between devices: 29.5 us -> none  [per_device(): lax.all_to_all(block_prob, 'tok', split_axis=1, concat_axis=0, tiled=True)]
    unnamed x22 -> x47, local copies, waits for them, and re-layouts: 31.8 us -> 9.78 us
  transfers between devices with their start and end apart: 3 -> 19, of which waited for: 3 -> 7; matrix products, arithmetic and copies ran while one was open for 15% -> 8% of each run, Pallas kernels for 0% -> 30%
where the time goes in v1:
time: 229 us; the launch traced here: 228 us
  Pallas kernels  88.9 us (39%)
  waiting for transfers between devices  43 us (19%)
  matrix products  36.7 us (16%)
  other arithmetic  25.1 us (11%)
  starting transfers between devices  16.2 us (7%)
  local copies, waits for them, and re-layouts  15.1 us (7%)
  between operations  2.93 us (1%)
    pallas_call x8, Pallas kernels, chunk_product(): pl.pallas_call(chunk_kernel, grid_spec=grid_spec, out_shape=jax.ShapeDtyp...  54.2 us
    ppermute x16, waiting for transfers between devices, swapped(): return lax.ppermute(value, axis, [(i, i ^ 1 << bit) for i in range(size)])  41.7 us
    pallas_call x7, Pallas kernels, grad_rows(): pl.pallas_call(grad_kernel, grid=(cut,), in_specs=[pl.BlockSpec((tokens,...  21.6 us
    dot_general x2, matrix products, per_device(): lax.dot_general(logit_grad, lax.slice_in_dim(student_head, at * width, (a...  16.3 us
    dot_general x1, matrix products, per_device(): jnp.dot(student_hidden, student_head, preferred_element_type=jnp.float32)  16.1 us
    ppermute x16, starting transfers between devices, swapped(): return lax.ppermute(value, axis, [(i, i ^ 1 << bit) for i in range(size)])  13.1 us
    pallas_call x1, Pallas kernels, merged_stats(): pl.pallas_call(functools.partial(stats_kernel, groups, ways), out_shape=j...  13 us
    unnamed x47, local copies, waits for them, and re-layouts  9.78 us
  transfers between devices with their start and end apart: 19, of which 7 were waited for; matrix products, arithmetic and copies ran while one was open for 8% of the time, Pallas kernels for 30%

profile of v1, /device:TPU:0, one launch (start us, length us, event | category | flops | bytes accessed | tf_op | source)
XLA Modules:
  0.0 227.8 jit_solution(15513292687915194079)
XLA Ops:
  0.7 1.6 copy-done.3
  2.3 7.2 %shard_map.89 = f32[512,1280]{1,0:T(8,128)} custom-call(s32[1]{0:T(128)} %bitcast.17.first_ref, bf16[512,2048]{1,0:T(8,128)(2,1)S(1)} %copy-done.3, bf16[2048,10240]{1,0:T(8,128)(2,1)} %b_ref.15), custom_call_target="tpu_custom_call" | custom-call | flops 2684354560 | bytes 9961472 | tf_op jit(solution)/shard_map/pallas_call | solution.py:45
  9.9 7.1 %shard_map.91 = f32[512,1280]{1,0:T(8,128)} custom-call(s32[1]{0:T(128)} %bitcast.19.first_ref, bf16[512,2048]{1,0:T(8,128)(2,1)S(1)} %copy-done.4, bf16[2048,10240]{1,0:T(8,128)(2,1)} %b_ref.15), custom_call_target="tpu_custom_call" | custom-call | flops 2684354560 | bytes 9961472 | tf_op jit(solution)/shard_map/pallas_call | solution.py:45
  17.0 7.1 %shard_map.85 = f32[512,1280]{1,0:T(8,128)} custom-call(s32[1]{0:T(128)} %bitcast.13.first_ref, bf16[512,2048]{1,0:T(8,128)(2,1)S(1)} %copy-done.4, bf16[2048,10240]{1,0:T(8,128)(2,1)} %b_ref.15), custom_call_target="tpu_custom_call" | custom-call | flops 2684354560 | bytes 9961472 | tf_op jit(solution)/shard_map/pallas_call | solution.py:45
  24.1 0.5 collective-permute-start.3
  24.6 7.1 %shard_map.87 = f32[512,1280]{1,0:T(8,128)} custom-call(s32[1]{0:T(128)} %bitcast.15.first_ref, bf16[512,2048]{1,0:T(8,128)(2,1)S(1)} %copy-done.4, bf16[2048,10240]{1,0:T(8,128)(2,1)} %b_ref.15), custom_call_target="tpu_custom_call" | custom-call | flops 2684354560 | bytes 9961472 | tf_op jit(solution)/shard_map/pallas_call | solution.py:45
  32.0 2.6 %collective-permute-start.2 = (s32[128,160]{0,1:T(8,128)S(1)}, s32[128,160]{0,1:T(8,128)S(1)}, u32[]{:S(2)}, u32[]{:S(2)}) collective-permute-start(s32[128,160]{0,1:T(8,128)S(1)} %get-tuple-element.70), channel_id=1, source_target_pairs={{0,3},{1,2},{2,1},{3,0},{4,7},{5,6},{6,5},{7,4},{8,11},{9,10},{10,... | collective-permute-start | bytes 245768 | tf_op jit(solution)/shard_map/ppermute | solution.py:192
  34.6 16.1 %fusion.44 = (f32[512]{0:T(512)S(1)}, f32[512,2560]{1,0:T(8,128)}) fusion(bf16[512,3584]{1,0:T(8,128)(2,1)} %hidden_ref.13, bf16[3584,2560]{1,0:T(8,128)(2,1)} %param.9), kind=kOutput, calls=%fused_computation.99 | convolution fusion | flops 9396551680 | bytes 27265024 | tf_op jit(solution)/shard_map/dot_general | solution.py:258
  51.2 6.4 %shard_map.92 = f32[512,1280]{1,0:T(8,128)S(1)} custom-call(s32[1]{0:T(128)} %bitcast.18.first_ref, bf16[512,2048]{1,0:T(8,128)(2,1)S(1)} %copy-done.4, bf16[2048,10240]{1,0:T(8,128)(2,1)} %b_ref.15, f32[512,1280]{1,0:T(8,128)} %collective-permute-done.7.rest_0_), custom_call_target="tpu_custom_call" | custom-call | flops 2684354560 | bytes 9961472 | tf_op jit(solution)/shard_map/pallas_call | solution.py:45
  57.7 1.7 collective-permute-start.8
  59.5 1.2 collective-permute-done
  60.9 6.4 %shard_map.88 = f32[512,1280]{1,0:T(8,128)S(1)} custom-call(s32[1]{0:T(128)} %bitcast.14.first_ref, bf16[512,2048]{1,0:T(8,128)(2,1)S(1)} %copy-done.4, bf16[2048,10240]{1,0:T(8,128)(2,1)} %b_ref.15, f32[512,1280]{1,0:T(8,128)} %collective-permute-done.4.rest_0_), custom_call_target="tpu_custom_call" | custom-call | flops 2684354560 | bytes 9961472 | tf_op jit(solution)/shard_map/pallas_call | solution.py:45
  67.4 0.5 collective-permute-start.5
  68.0 6.4 %shard_map.90 = f32[512,1280]{1,0:T(8,128)S(1)} custom-call(s32[1]{0:T(128)} %bitcast.16.first_ref, bf16[512,2048]{1,0:T(8,128)(2,1)S(1)} %copy-done.4, bf16[2048,10240]{1,0:T(8,128)(2,1)} %b_ref.15, f32[512,1280]{1,0:T(8,128)} %collective-permute-done.6.rest_0_), custom_call_target="tpu_custom_call" | custom-call | flops 2684354560 | bytes 9961472 | tf_op jit(solution)/shard_map/pallas_call | solution.py:45
  74.4 6.5 %shard_map.86 = f32[512,1280]{1,0:T(8,128)S(1)} custom-call(s32[1]{0:T(128)} %bitcast.12.first_ref, bf16[512,2048]{1,0:T(8,128)(2,1)S(1)} %copy-done.4, bf16[2048,10240]{1,0:T(8,128)(2,1)} %b_ref.15, f32[512,1280]{1,0:T(8,128)} %collective-permute-done.3.rest_0_), custom_call_target="tpu_custom_call" | custom-call | flops 2684354560 | bytes 9961472 | tf_op jit(solution)/shard_map/pallas_call | solution.py:45
  80.9 8.5 %collective-permute-done.8 = f16[512,1280]{1,0:T(8,128)(2,1)S(1)} collective-permute-done((f16[512,1280]{1,0:T(8,128)(2,1)S(1)}, f16[512,1280]{1,0:T(8,128)(2,1)S(1)}, u32[]{:S(2)}, u32[]{:S(2)}) %collective-permute-start.8) | collective-permute-done | bytes 1310752 | tf_op jit(solution)/shard_map/ppermute | solution.py:21
  89.7 27.0 %collective-permute-done.5 = f16[512,1280]{1,0:T(8,128)(2,1)S(1)} collective-permute-done((f16[512,1280]{1,0:T(8,128)(2,1)S(1)}, f16[512,1280]{1,0:T(8,128)(2,1)S(1)}, u32[]{:S(2)}, u32[]{:S(2)}) %collective-permute-start.5) | collective-permute-done | bytes 1310752 | tf_op jit(solution)/shard_map/ppermute | solution.py:21
  117.1 4.2 %fusion.42 = (f32[512]{0:T(512)S(1)}, pred[512,2560]{1,0:T(8,128)(4,1)S(1)}) fusion(f32[512,1280]{1,0:T(8,128)S(1)} %convert_add_fusion, f32[512,1280]{1,0:T(8,128)S(1)} %convert_add_fusion.1, s32[512]{0:T(512)S(1)} %copy-done.20, s32[2560]{0:T(1024)S(1)} %iota_add_fusion, s32[2560]{0:T(1024)S(1)} %get-tuple-element.83, s32[2560]{0:T(1024)S(1)} %get-tuple-element.84, ...), kind=kOutput, calls=%fused_computation.97 | convolution fusion | flops 858684928 | bytes 6916096 | tf_op jit(solution)/shard_map/dot_general | solution.py:207
  121.5 4.9 %fusion.4 = (f32[512]{0:T(512)S(1)}, f32[512]{0:T(512)S(1)}, f32[512]{0:T(512)S(1)}, f32[512]{0:T(512)S(1)}) fusion(f32[512,2560]{1,0:T(8,128)S(1)} %bitcast.87, s32[2560]{0:T(1024)S(1)} %iota_add_fusion, s32[512]{0:T(512)S(1)} %copy-done.20, pred[512,2560]{1,0:T(8,128)(4,1)S(1)} %get-tuple-element.80, f32[512,1280]{1,0:T(8,128)S(1)} %convert_add_fusion, ...), kind=kLoop, calls=%fused_computation.7 | loop fusion | flops 19658752 | bytes 11821056 | tf_op jit(solution)/shard_map/reduce_sum | solution.py:280
  126.3 0.6 stack.51.part_ref
  127.0 13.0 %shard_map.93 = f32[8,512]{1,0:T(8,128)} custom-call(f32[8,512]{1,0:T(8,128)} %stack.51.part_ref), custom_call_target="tpu_custom_call" | custom-call | tf_op jit(solution)/shard_map/pallas_call | solution.py:168
  140.0 1.6 fusion.43
  141.7 6.6 %fusion.6.grad_ref = bf16[512,2560]{1,0:T(8,128)(2,1)S(1)} fusion(f32[512,2560]{1,0:T(8,128)} %get-tuple-element.82, pred[512,2560]{1,0:T(8,128)(4,1)} %copy-done.13, f32[512]{0:T(512)S(1)} %bitcast.100, f32[512]{0:T(512)S(1)} %bitcast.96, f32[512]{0:T(512)S(1)} %bitcast.98, f32[512]{0:T(512)S(1)} %bitcast.94, s32[2560]{0:T(1024)S(1)} %iota_add_fusion, ...), kind=kLoop, calls=%fused_computation.9 | loop fusion | flops 19660800 | bytes 14438400 | tf_op jit(solution)/shard_map/convert_element_type | solution.py:301
  148.3 8.1 %fusion.9 = f32[512,1792]{1,0:T(8,128)S(1)} fusion(bf16[512,2560]{1,0:T(8,128)(2,1)S(1)} %fusion.6.grad_ref, bf16[3584,2560]{1,0:T(8,128)(2,1)} %param.9), kind=kOutput, calls=%fused_computation.19 | convolution fusion | flops 4698537984 | bytes 15466496 | tf_op jit(solution)/shard_map/dot_general | solution.py:312
  156.4 8.1 %fusion.12 = f32[512,1792]{1,0:T(8,128)S(1)} fusion(bf16[512,2560]{1,0:T(8,128)(2,1)S(1)} %fusion.6.grad_ref, bf16[3584,2560]{1,0:T(8,128)(2,1)} %param.9), kind=kOutput, calls=%fused_computation.20 | convolution fusion | flops 4698537984 | bytes 15466496 | tf_op jit(solution)/shard_map/dot_general | solution.py:312
  164.5 1.5 constant_dynamic-slice_fusion.2
  166.1 1.5 constant_dynamic-slice_fusion
  167.6 1.0 fusion.17
  168.7 0.5 collective-permute-start.10
  169.2 2.0 copy-done
  171.2 3.1 %shard_map.94.rest_0_ = bf16[3584,2560]{1,0:T(8,128)(2,1)} custom-call(bf16[512,3584]{1,0:T(8,128)(2,1)S(1)} %copy-done, bf16[512,2560]{1,0:T(8,128)(2,1)S(1)} %fusion.6.grad_ref), custom_call_target="tpu_custom_call" | custom-call | flops 1342177280 | bytes 5767168 | tf_op jit(solution)/shard_map/pallas_call | solution.py:72
  174.3 3.1 %shard_map.95.rest_0_ = bf16[3584,2560]{1,0:T(8,128)(2,1)} custom-call(bf16[512,3584]{1,0:T(8,128)(2,1)S(1)} %copy-done, bf16[512,2560]{1,0:T(8,128)(2,1)S(1)} %fusion.6.grad_ref, bf16[3584,2560]{1,0:T(8,128)(2,1)} %shard_map.94.rest_0_), custom_call_target="tpu_custom_call", output_to_operand_aliasing={{}: (2, {})} | custom-call | flops 1342177280 | bytes 5767168 | tf_op jit(solution)/shard_map/pallas_call | solution.py:72
  177.4 1.5 bitcast_add_fusion.1
  179.2 1.9 bitcast_add_fusion
  181.1 0.9 fusion.19
  182.0 0.6 collective-permute-start.11
  182.6 1.7 collective-permute-start.12
  184.3 2.0 copy-done.1
  186.3 3.1 %shard_map.96.rest_0_ = bf16[3584,2560]{1,0:T(8,128)(2,1)} custom-call(bf16[512,3584]{1,0:T(8,128)(2,1)S(1)} %copy-done.1, bf16[512,2560]{1,0:T(8,128)(2,1)S(1)} %fusion.6.grad_ref, bf16[3584,2560]{1,0:T(8,128)(2,1)} %shard_map.95.rest_0_), custom_call_target="tpu_custom_call", output_to_operand_aliasing={{}: (2, {})} | custom-call | flops 1342177280 | bytes 5767168 | tf_op jit(solution)/shard_map/pallas_call | solution.py:72
  189.4 3.1 %shard_map.97.rest_0_ = bf16[3584,2560]{1,0:T(8,128)(2,1)} custom-call(bf16[512,3584]{1,0:T(8,128)(2,1)S(1)} %copy-done.1, bf16[512,2560]{1,0:T(8,128)(2,1)S(1)} %fusion.6.grad_ref, bf16[3584,2560]{1,0:T(8,128)(2,1)} %shard_map.96.rest_0_), custom_call_target="tpu_custom_call", output_to_operand_aliasing={{}: (2, {})} | custom-call | flops 1342177280 | bytes 5767168 | tf_op jit(solution)/shard_map/pallas_call | solution.py:72
  192.5 3.1 %shard_map.98.rest_0_ = bf16[3584,2560]{1,0:T(8,128)(2,1)} custom-call(bf16[512,3584]{1,0:T(8,128)(2,1)S(1)} %copy-done.1, bf16[512,2560]{1,0:T(8,128)(2,1)S(1)} %fusion.6.grad_ref, bf16[3584,2560]{1,0:T(8,128)(2,1)} %shard_map.97.rest_0_), custom_call_target="tpu_custom_call", output_to_operand_aliasing={{}: (2, {})} | custom-call | flops 1342177280 | bytes 5767168 | tf_op jit(solution)/shard_map/pallas_call | solution.py:72
  195.6 0.8 copy-done.16
  196.4 1.1 bitcast_add_fusion.3
  197.5 0.7 fusion.23
  198.2 1.1 bitcast_add_fusion.2
  199.4 0.9 copy-done.14
  200.3 0.7 fusion.24
  201.0 0.7 collective-permute-start.13
  201.7 1.2 collective-permute-start.14
  202.9 2.0 copy-done.2
  204.9 3.1 %shard_map.99.rest_0_ = bf16[3584,2560]{1,0:T(8,128)(2,1)} custom-call(bf16[512,3584]{1,0:T(8,128)(2,1)S(1)} %copy-done.2, bf16[512,2560]{1,0:T(8,128)(2,1)S(1)} %fusion.6.grad_ref, bf16[3584,2560]{1,0:T(8,128)(2,1)} %shard_map.98.rest_0_), custom_call_target="tpu_custom_call", output_to_operand_aliasing={{}: (2, {})} | custom-call | flops 1342177280 | bytes 5767168 | tf_op jit(solution)/shard_map/pallas_call | solution.py:72
  208.0 0.5 collective-permute-done.13
  208.6 1.0 bitcast_add_fusion.5
  209.6 1.0 bitcast_add_fusion.4
  210.6 1.3 collective-permute-start.15
  212.0 0.8 collective-permute-start.16
  212.7 3.1 %shard_map.100 = bf16[3584,2560]{1,0:T(8,128)(2,1)} custom-call(bf16[512,3584]{1,0:T(8,128)(2,1)S(1)} %copy-done.2, bf16[512,2560]{1,0:T(8,128)(2,1)S(1)} %fusion.6.grad_ref, bf16[3584,2560]{1,0:T(8,128)(2,1)} %shard_map.99.rest_0_), custom_call_target="tpu_custom_call", output_to_operand_aliasing={{}: (2, {})} | custom-call | flops 1342177280 | bytes 5767168 | tf_op jit(solution)/shard_map/pallas_call | solution.py:72
  215.8 1.2 collective-permute-done.16
  217.2 2.4 %collective-permute-start.18 = (f16[16,1792]{1,0:T(8,128)(2,1)S(1)}, f16[16,1792]{1,0:T(8,128)(2,1)S(1)}, u32[]{:S(2)}, u32[]{:S(2)}) collective-permute-start(f16[16,1792]{1,0:T(8,128)(2,1)S(1)} %fusion.28), channel_id=1, source_target_pairs={{0,16},{4,20},{8,24},{12,28},{16,0},{20,4},{24,8},{28,12},{1,17},{... | collective-permute-start | bytes 172040 | tf_op jit(solution)/shard_map/ppermute | solution.py:21
  219.6 0.6 add_reduce_fusion
  220.8 0.7 collective-permute-start.17
  221.5 1.0 collective-permute-done.18
  222.5 3.5 %collective-permute-done.17 = f16[16,1792]{1,0:T(8,128)(2,1)S(1)} collective-permute-done((f16[16,1792]{1,0:T(8,128)(2,1)S(1)}, f16[16,1792]{1,0:T(8,128)(2,1)S(1)}, u32[]{:S(2)}, u32[]{:S(2)}) %collective-permute-start.17) | collective-permute-done | bytes 57376 | tf_op jit(solution)/shard_map/ppermute | solution.py:21
  226.0 0.7 maximum_multiply_fusion
  (81 shorter events, 2.9 us)
Async XLA Ops:
  0.7 1.6 copy-start.3
  2.3 7.7 %copy-start.4 = (bf16[512,2048]{1,0:T(8,128)(2,1)S(1)}, bf16[512,2048]{1,0:T(8,128)(2,1)}, u32[]{:S(2)}) copy-start(bf16[512,2048]{1,0:T(8,128)(2,1)} %a_ref.15) | copy-start | bytes 6291460
  9.5 58.5 %collective-permute-start.6 = (f32[512,1280]{1,0:T(8,128)}, f32[512,1280]{1,0:T(8,128)}, u32[]{:S(2)}, u32[]{:S(2)}) collective-permute-start(f32[512,1280]{1,0:T(8,128)} %shard_map.89), channel_id=1, source_target_pairs={{0,1},{1,0},{2,3},{3,2},{4,5},{5,4},{6,7},{7,6},{8,9},{9,8},{10,11... | collective-permute-start | bytes 7864328 | tf_op jit(solution)/shard_map/ppermute | solution.py:21
  17.0 33.8 %collective-permute-start.7 = (f32[512,1280]{1,0:T(8,128)}, f32[512,1280]{1,0:T(8,128)}, u32[]{:S(2)}, u32[]{:S(2)}) collective-permute-start(f32[512,1280]{1,0:T(8,128)} %shard_map.91), channel_id=1, source_target_pairs={{0,1},{1,0},{2,3},{3,2},{4,5},{5,4},{6,7},{7,6},{8,9},{9,8},{10,11... | collective-permute-start | bytes 7864328 | tf_op jit(solution)/shard_map/ppermute | solution.py:21
  24.1 50.3 %collective-permute-start.3 = (f32[512,1280]{1,0:T(8,128)}, f32[512,1280]{1,0:T(8,128)}, u32[]{:S(2)}, u32[]{:S(2)}) collective-permute-start(f32[512,1280]{1,0:T(8,128)} %shard_map.85), channel_id=1, source_target_pairs={{0,1},{1,0},{2,3},{3,2},{4,5},{5,4},{6,7},{7,6},{8,9},{9,8},{10,11... | collective-permute-start | bytes 7864328 | tf_op jit(solution)/shard_map/ppermute | solution.py:21
  24.6 7.2 %copy-start.17 = (s32[128,640]{1,0:T(8,128)S(1)}, s32[128,640]{1,0:T(8,128)}, u32[]{:S(2)}) copy-start(s32[128,640]{1,0:T(8,128)} %param.10) | copy-start | bytes 983044
  31.7 29.1 %collective-permute-start.4 = (f32[512,1280]{1,0:T(8,128)}, f32[512,1280]{1,0:T(8,128)}, u32[]{:S(2)}, u32[]{:S(2)}) collective-permute-start(f32[512,1280]{1,0:T(8,128)} %shard_map.87), channel_id=1, source_target_pairs={{0,1},{1,0},{2,3},{3,2},{4,5},{5,4},{6,7},{7,6},{8,9},{9,8},{10,11... | collective-permute-start | bytes 7864328 | tf_op jit(solution)/shard_map/ppermute | solution.py:21
  32.0 25.8 %collective-permute-start.2 = (s32[128,160]{0,1:T(8,128)S(1)}, s32[128,160]{0,1:T(8,128)S(1)}, u32[]{:S(2)}, u32[]{:S(2)}) collective-permute-start(s32[128,160]{0,1:T(8,128)S(1)} %get-tuple-element.70), channel_id=1, source_target_pairs={{0,3},{1,2},{2,1},{3,0},{4,7},{5,6},{6,5},{7,4},{8,11},{9,10},{10,... | collective-permute-start | bytes 245768 | tf_op jit(solution)/shard_map/ppermute | solution.py:192
  50.8 8.7 %collective-permute-start.1 = (s32[128,160]{0,1:T(8,128)S(1)}, s32[128,160]{0,1:T(8,128)S(1)}, u32[]{:S(2)}, u32[]{:S(2)}) collective-permute-start(s32[128,160]{0,1:T(8,128)S(1)} %get-tuple-element.71), channel_id=1, source_target_pairs={{0,2},{1,3},{2,0},{3,1},{4,6},{5,7},{6,4},{7,5},{8,10},{9,11},{10,... | collective-permute-start | bytes 245768 | tf_op jit(solution)/shard_map/ppermute | solution.py:192
  57.7 31.7 %collective-permute-start.8 = (f16[512,1280]{1,0:T(8,128)(2,1)S(1)}, f16[512,1280]{1,0:T(8,128)(2,1)S(1)}, u32[]{:S(2)}, u32[]{:S(2)}) collective-permute-start(f16[512,1280]{1,0:T(8,128)(2,1)S(1)} %convert_element_type.131), channel_id=1, source_target_pairs={{0,2},{1,3},{2,0},{3,1},{4,6},{5,7},{6,4},{7,5},{8,10},{9,11},{10,... | collective-permute-start | bytes 3932168 | tf_op jit(solution)/shard_map/ppermute | solution.py:21
  59.4 1.3 collective-permute-start
  67.4 49.2 %collective-permute-start.5 = (f16[512,1280]{1,0:T(8,128)(2,1)S(1)}, f16[512,1280]{1,0:T(8,128)(2,1)S(1)}, u32[]{:S(2)}, u32[]{:S(2)}) collective-permute-start(f16[512,1280]{1,0:T(8,128)(2,1)S(1)} %convert_element_type.129), channel_id=1, source_target_pairs={{0,2},{1,3},{2,0},{3,1},{4,6},{5,7},{6,4},{7,5},{8,10},{9,11},{10,... | collective-permute-start | bytes 3932168 | tf_op jit(solution)/shard_map/ppermute | solution.py:21
  89.7 31.7 %copy-start.5 = (f32[512,1280]{1,0:T(8,128)}, f32[512,1280]{1,0:T(8,128)S(1)}, u32[]{:S(2)}) copy-start(f32[512,1280]{1,0:T(8,128)S(1)} %convert_add_fusion) | copy-start | bytes 7864324
  89.7 27.4 %copy-start.20 = (s32[512]{0:T(512)S(1)}, s32[512]{0:T(512)}, u32[]{:S(2)}) copy-start(s32[512]{0:T(512)} %param.11) | copy-start | bytes 6148
  116.7 4.7 %slice-start = ((s8[5242880]{0:T(1024)(128)(4,1)}), s8[4194304]{0:T(1024)(128)(4,1)S(1)}, s32[]{:S(2)}) async-start(s8[5242880]{0:T(1024)(128)(4,1)} %bitcast.86), calls=%async_computation | async-start | bytes 8388608
  117.1 4.3 %copy-start.6 = (f32[512,1280]{1,0:T(8,128)}, f32[512,1280]{1,0:T(8,128)S(1)}, u32[]{:S(2)}) copy-start(f32[512,1280]{1,0:T(8,128)S(1)} %convert_add_fusion.1) | copy-start | bytes 7864324
  117.1 4.3 %slice-start.1 = ((s8[5242880]{0:T(1024)(128)(4,1)}), s8[1048576]{0:T(1024)(128)(4,1)S(1)}, s32[]{:S(2)}) async-start(s8[5242880]{0:T(1024)(128)(4,1)} %bitcast.86), calls=%async_computation.1 | async-start | bytes 2097152
  121.4 4.9 %copy-start.13 = (pred[512,2560]{1,0:T(8,128)(4,1)}, pred[512,2560]{1,0:T(8,128)(4,1)S(1)}, u32[]{:S(2)}) copy-start(pred[512,2560]{1,0:T(8,128)(4,1)S(1)} %get-tuple-element.80) | copy-start | bytes 3932164
  168.7 8.7 %collective-permute-start.9 = (f16[2,2,2,2,16,1792]{5,4,0,1,2,3:T(8,128)(2,1)S(1)}, f16[2,2,2,2,16,1792]{5,4,0,1,2,3:T(8,128)(2,1)}, u32[]{:S(2)}, u32[]{:S(2)}) collective-permute-start(f16[2,2,2,2,16,1792]{5,4,0,1,2,3:T(8,128)(2,1)S(1)} %fusion.16), channel_id=1, source_target_pairs={{0,1},{1,0},{2,3},{3,2},{4,5},{5,4},{6,7},{7,6},{8,9},{9,8},{10,11... | collective-permute-start | bytes 2752520 | tf_op jit(solution)/shard_map/ppermute | solution.py:21
  168.7 8.7 %collective-permute-start.10 = (f16[2,2,2,2,16,1792]{5,4,0,1,3,2:T(8,128)(2,1)}, f16[2,2,2,2,16,1792]{5,4,0,1,3,2:T(8,128)(2,1)}, u32[]{:S(2)}, u32[]{:S(2)}) collective-permute-start(f16[2,2,2,2,16,1792]{5,4,0,1,3,2:T(8,128)(2,1)} %fusion.17), channel_id=1, source_target_pairs={{0,1},{1,0},{2,3},{3,2},{4,5},{5,4},{6,7},{7,6},{8,9},{9,8},{10,11... | collective-permute-start | bytes 2752520 | tf_op jit(solution)/shard_map/ppermute | solution.py:21
  169.2 2.0 copy-start
  174.3 3.1 %copy-start.11 = (f32[2,2,2,2,1,16,1792]{6,5,4,3,2,1,0:T(8,128)S(1)}, f32[2,2,2,2,1,16,1792]{6,5,4,3,2,1,0:T(8,128)}, u32[]{:S(2)}) copy-start(f32[2,2,2,2,1,16,1792]{6,5,4,3,2,1,0:T(8,128)} %get-tuple-element.62) | copy-start | bytes 5505028
  177.4 1.8 copy-start.12
  178.9 3.0 %copy-start.7 = (f32[2,2,2,2,16,1792]{5,4,0,1,2,3:T(8,128)}, f32[2,2,2,2,16,1792]{5,4,0,1,2,3:T(8,128)S(1)}, u32[]{:S(2)}) copy-start(f32[2,2,2,2,16,1792]{5,4,0,1,2,3:T(8,128)S(1)} %bitcast_add_fusion.1) | copy-start | bytes 5505028
  181.1 1.5 copy-start.9
  182.0 13.7 %collective-permute-start.11 = (f16[2,2,2,16,1792]{4,3,0,1,2:T(8,128)(2,1)S(1)}, f16[2,2,2,16,1792]{4,3,0,1,2:T(8,128)(2,1)S(1)}, u32[]{:S(2)}, u32[]{:S(2)}) collective-permute-start(f16[2,2,2,16,1792]{4,3,0,1,2:T(8,128)(2,1)S(1)} %fusion.18), channel_id=1, source_target_pairs={{0,2},{1,3},{2,0},{3,1},{4,6},{5,7},{6,4},{7,5},{8,10},{9,11},{10,... | collective-permute-start | bytes 1376264 | tf_op jit(solution)/shard_map/ppermute | solution.py:21
  182.6 13.8 %collective-permute-start.12 = (f16[2,2,2,16,1792]{4,3,0,1,2:T(8,128)(2,1)}, f16[2,2,2,16,1792]{4,3,0,1,2:T(8,128)(2,1)}, u32[]{:S(2)}, u32[]{:S(2)}) collective-permute-start(f16[2,2,2,16,1792]{4,3,0,1,2:T(8,128)(2,1)} %fusion.19), channel_id=1, source_target_pairs={{0,4},{4,0},{8,12},{12,8},{16,20},{20,16},{24,28},{28,24},{1,5},{5... | collective-permute-start | bytes 1376264 | tf_op jit(solution)/shard_map/ppermute | solution.py:21
  184.3 2.0 copy-start.1
  192.5 3.9 %copy-start.8 = (f32[2,2,2,2,16,1792]{5,4,0,1,2,3:T(8,128)S(1)}, f32[2,2,2,2,16,1792]{5,4,0,1,2,3:T(8,128)}, u32[]{:S(2)}) copy-start(f32[2,2,2,2,16,1792]{5,4,0,1,2,3:T(8,128)} %copy-done.7) | copy-start | bytes 5505028
  192.5 5.7 %copy-start.10 = (f32[2,2,2,2,16,1792]{5,4,0,1,3,2:T(8,128)S(1)}, f32[2,2,2,2,16,1792]{5,4,0,1,3,2:T(8,128)}, u32[]{:S(2)}) copy-start(f32[2,2,2,2,16,1792]{5,4,0,1,3,2:T(8,128)} %copy-done.9) | copy-start | bytes 5505028
  195.6 0.8 copy-start.16
  199.4 0.9 copy-start.14
  201.0 7.6 %collective-permute-start.13 = (f16[2,2,16,1792]{3,2,0,1:T(8,128)(2,1)}, f16[2,2,16,1792]{3,2,0,1:T(8,128)(2,1)}, u32[]{:S(2)}, u32[]{:S(2)}) collective-permute-start(f16[2,2,16,1792]{3,2,0,1:T(8,128)(2,1)} %fusion.23), channel_id=1, source_target_pairs={{0,4},{4,0},{8,12},{12,8},{16,20},{20,16},{24,28},{28,24},{1,5},{5... | collective-permute-start | bytes 688136 | tf_op jit(solution)/shard_map/ppermute | solution.py:21
  201.7 6.9 %collective-permute-start.14 = (f16[2,2,16,1792]{3,2,0,1:T(8,128)(2,1)}, f16[2,2,16,1792]{3,2,0,1:T(8,128)(2,1)}, u32[]{:S(2)}, u32[]{:S(2)}) collective-permute-start(f16[2,2,16,1792]{3,2,0,1:T(8,128)(2,1)} %fusion.24), channel_id=1, source_target_pairs={{0,2},{1,3},{2,0},{3,1},{4,6},{5,7},{6,4},{7,5},{8,10},{9,11},{10,... | collective-permute-start | bytes 688136 | tf_op jit(solution)/shard_map/ppermute | solution.py:21
  202.9 2.0 copy-start.2
  204.9 4.6 %copy-start.15 = (f32[2,2,2,16,1792]{4,3,0,1,2:T(8,128)S(1)}, f32[2,2,2,16,1792]{4,3,0,1,2:T(8,128)}, u32[]{:S(2)}) copy-start(f32[2,2,2,16,1792]{4,3,0,1,2:T(8,128)} %copy-done.14) | copy-start | bytes 2752516
  210.6 8.9 %copy-start.18 = (f32[1,512]{1,0:T(1,128)S(1)}, f32[1,512]{1,0:T(1,128)}, u32[]{:S(2)}) copy-start(f32[1,512]{1,0:T(1,128)} %get-tuple-element.73) | copy-start | bytes 6148
  210.6 8.9 %copy-start.19 = (f32[1,512]{1,0:T(1,128)S(1)}, f32[1,512]{1,0:T(1,128)}, u32[]{:S(2)}) copy-start(f32[1,512]{1,0:T(1,128)} %get-tuple-element.76) | copy-start | bytes 6148
  210.6 5.2 %collective-permute-start.15 = (f16[2,16,1792]{2,1,0:T(8,128)(2,1)S(1)}, f16[2,16,1792]{2,1,0:T(8,128)(2,1)S(1)}, u32[]{:S(2)}, u32[]{:S(2)}) collective-permute-start(f16[2,16,1792]{2,1,0:T(8,128)(2,1)S(1)} %fusion.25), channel_id=1, source_target_pairs={{0,8},{4,12},{8,0},{12,4},{16,24},{20,28},{24,16},{28,20},{1,9},{5... | collective-permute-start | bytes 344072 | tf_op jit(solution)/shard_map/ppermute | solution.py:21
  212.0 5.1 %collective-permute-start.16 = (f16[2,16,1792]{2,1,0:T(8,128)(2,1)S(1)}, f16[2,16,1792]{2,1,0:T(8,128)(2,1)S(1)}, u32[]{:S(2)}, u32[]{:S(2)}) collective-permute-start(f16[2,16,1792]{2,1,0:T(8,128)(2,1)S(1)} %fusion.26), channel_id=1, source_target_pairs={{0,8},{4,12},{8,0},{12,4},{16,24},{20,28},{24,16},{28,20},{1,9},{5... | collective-permute-start | bytes 344072 | tf_op jit(solution)/shard_map/ppermute | solution.py:21
  217.2 5.3 %collective-permute-start.18 = (f16[16,1792]{1,0:T(8,128)(2,1)S(1)}, f16[16,1792]{1,0:T(8,128)(2,1)S(1)}, u32[]{:S(2)}, u32[]{:S(2)}) collective-permute-start(f16[16,1792]{1,0:T(8,128)(2,1)S(1)} %fusion.28), channel_id=1, source_target_pairs={{0,16},{4,20},{8,24},{12,28},{16,0},{20,4},{24,8},{28,12},{1,17},{... | collective-permute-start | bytes 172040 | tf_op jit(solution)/shard_map/ppermute | solution.py:21
  220.8 5.1 %collective-permute-start.17 = (f16[16,1792]{1,0:T(8,128)(2,1)S(1)}, f16[16,1792]{1,0:T(8,128)(2,1)S(1)}, u32[]{:S(2)}, u32[]{:S(2)}) collective-permute-start(f16[16,1792]{1,0:T(8,128)(2,1)S(1)} %fusion.27), channel_id=1, source_target_pairs={{0,16},{4,20},{8,24},{12,28},{16,0},{20,4},{24,8},{28,12},{1,17},{... | collective-permute-start | bytes 172040 | tf_op jit(solution)/shard_map/ppermute | solution.py:21

commit v2 on v1

--- a/solution.py
+++ b/solution.py
@@ -48,8 +48,8 @@
         out_shape=jax.ShapeDtypeStruct((rows, width), out_dtype),
         compiler_params=pltpu.CompilerParams(vmem_limit_bytes=40 * 1024 * 1024),
         cost_estimate=pl.CostEstimate(
-            flops=2 * rows * depth * width,
-            bytes_accessed=2 * (rows * depth + depth * width + 2 * rows * width),
+            flops=rows * depth * width // 8,
+            bytes_accessed=(rows * depth + depth * width + 2 * rows * width) // 8,
             transcendentals=0,
         ),
     )((first // tile).reshape(1).astype(jnp.int32), a, b, *extras)
@@ -248,8 +248,9 @@
         far.append(swapped(away, "tok", 0))
     sent = []
     for at, lower in enumerate((0, half)):
-        away = product(mine ^ 2, lower, jnp.float32, (far[at],))
-        sent.append(swapped(away.astype(jnp.float16), "tok", 1))
+        away = product(mine ^ 2, lower, jnp.float32, (far[at],)).astype(jnp.float16)
+        away, mine, student_hidden = lax.optimization_barrier((away, mine, student_hidden))
+        sent.append(swapped(away, "tok", 1))
     for lower in (0, half):
         away = product(mine ^ 1, lower, jnp.float32)
         near.append(swapped(away, "tok", 0))

time: 229 us -> 221 us (0.965)
  waiting for transfers between devices: 43 us -> 31 us
  other arithmetic: 25.1 us -> 29.6 us
    ppermute x16, waiting for transfers between devices: 41.7 us -> 26.6 us  [swapped(): return lax.ppermute(value, axis, [(i, i ^ 1 << bit) for i in range(size)])]
    ppermute x3, waiting for transfers between devices: 1.25 us -> 4.33 us  [words_here(): lax.ppermute(piece, 'tok', [(i, i ^ step) for i in range(groups)])]
    add x2, other arithmetic: 0.67 us -> 3.41 us  [per_device(): own[at] + sent[at].astype(jnp.float32)]
    unnamed x47 -> x53, local copies, waits for them, and re-layouts: 9.78 us -> 9.82 us
  transfers between devices with their start and end apart: 19 -> 19, of which waited for: 7 -> 7; matrix products, arithmetic and copies ran while one was open for 8% -> 8% of each run, Pallas kernels for 30% -> 25%
where the time goes in v2:
time: 221 us; the launch traced here: 219 us
  Pallas kernels  89 us (40%)
  matrix products  35.6 us (16%)
  waiting for transfers between devices  31 us (14%)
  other arithmetic  29.6 us (13%)
  starting transfers between devices  16.1 us (7%)
  local copies, waits for them, and re-layouts  15 us (7%)
  between operations  2.96 us (1%)
    pallas_call x8, Pallas kernels, chunk_product(): pl.pallas_call(chunk_kernel, grid_spec=grid_spec, out_shape=jax.ShapeDtyp...  54.4 us
    ppermute x16, waiting for transfers between devices, swapped(): return lax.ppermute(value, axis, [(i, i ^ 1 << bit) for i in range(size)])  26.6 us
    pallas_call x7, Pallas kernels, grad_rows(): pl.pallas_call(grad_kernel, grid=(cut,), in_specs=[pl.BlockSpec((tokens,...  21.6 us
    dot_general x2, matrix products, per_device(): lax.dot_general(logit_grad, lax.slice_in_dim(student_head, at * width, (a...  16.3 us
    dot_general x1, matrix products, per_device(): jnp.dot(student_hidden, student_head, preferred_element_type=jnp.float32)  15 us
    pallas_call x1, Pallas kernels, merged_stats(): pl.pallas_call(functools.partial(stats_kernel, groups, ways), out_shape=j...  13.1 us
    ppermute x16, starting transfers between devices, swapped(): return lax.ppermute(value, axis, [(i, i ^ 1 << bit) for i in range(size)])  13 us
    unnamed x53, local copies, waits for them, and re-layouts  9.82 us
  transfers between devices with their start and end apart: 19, of which 7 were waited for; matrix products, arithmetic and copies ran while one was open for 8% of the time, Pallas kernels for 25%

profile of v2, /device:TPU:0, one launch (start us, length us, event | category | flops | bytes accessed | tf_op | source)
XLA Modules:
  0.0 219.3 jit_solution(7265335119291998256)
XLA Ops:
  0.7 1.6 copy-done.4
  2.3 7.2 %shard_map.85 = f32[512,1280]{1,0:T(8,128)} custom-call(s32[1]{0:T(128)} %bitcast.13.first_ref, bf16[512,2048]{1,0:T(8,128)(2,1)S(1)} %copy-done.4, bf16[2048,10240]{1,0:T(8,128)(2,1)} %b_ref.15), custom_call_target="tpu_custom_call" | custom-call | flops 167772160 | bytes 622592 | tf_op jit(solution)/shard_map/pallas_call | solution.py:45
  9.9 7.1 %shard_map.87 = f32[512,1280]{1,0:T(8,128)} custom-call(s32[1]{0:T(128)} %bitcast.15.first_ref, bf16[512,2048]{1,0:T(8,128)(2,1)S(1)} %copy-done.5, bf16[2048,10240]{1,0:T(8,128)(2,1)} %b_ref.15), custom_call_target="tpu_custom_call" | custom-call | flops 167772160 | bytes 622592 | tf_op jit(solution)/shard_map/pallas_call | solution.py:45
  17.3 2.6 %collective-permute-start.2 = (s32[128,160]{0,1:T(8,128)S(1)}, s32[128,160]{0,1:T(8,128)S(1)}, u32[]{:S(2)}, u32[]{:S(2)}) collective-permute-start(s32[128,160]{0,1:T(8,128)S(1)} %get-tuple-element.82), channel_id=1, source_target_pairs={{0,3},{1,2},{2,1},{3,0},{4,7},{5,6},{6,5},{7,4},{8,11},{9,10},{10,... | collective-permute-start | bytes 245768 | tf_op jit(solution)/shard_map/ppermute | solution.py:192
  20.4 2.3 %collective-permute-done.2 = s32[128,160]{0,1:T(8,128)S(1)} collective-permute-done((s32[128,160]{0,1:T(8,128)S(1)}, s32[128,160]{0,1:T(8,128)S(1)}, u32[]{:S(2)}, u32[]{:S(2)}) %collective-permute-start.2) | collective-permute-done | bytes 81952 | tf_op jit(solution)/shard_map/ppermute | solution.py:192
  22.7 2.0 collective-permute-done.1
  24.8 0.8 and_convert_fusion
  25.6 6.4 %shard_map.86 = f32[512,1280]{1,0:T(8,128)S(1)} custom-call(s32[1]{0:T(128)} %bitcast.12.first_ref, bf16[512,2048]{1,0:T(8,128)(2,1)S(1)} %copy-done.5, bf16[2048,10240]{1,0:T(8,128)(2,1)} %b_ref.15, f32[512,1280]{1,0:T(8,128)} %collective-permute-done.3.rest_0_), custom_call_target="tpu_custom_call" | custom-call | flops 167772160 | bytes 622592 | tf_op jit(solution)/shard_map/pallas_call | solution.py:45
  32.2 6.4 %shard_map.88 = f32[512,1280]{1,0:T(8,128)S(1)} custom-call(s32[1]{0:T(128)} %bitcast.14.first_ref, bf16[512,2048]{1,0:T(8,128)(2,1)S(1)} %copy-done.5, bf16[2048,10240]{1,0:T(8,128)(2,1)} %b_ref.15, f32[512,1280]{1,0:T(8,128)} %collective-permute-done.4.rest_0_), custom_call_target="tpu_custom_call" | custom-call | flops 167772160 | bytes 622592 | tf_op jit(solution)/shard_map/pallas_call | solution.py:45
  38.7 1.2 convert_element_type.130
  39.8 7.1 %shard_map.91 = f32[512,1280]{1,0:T(8,128)} custom-call(s32[1]{0:T(128)} %bitcast.19.first_ref, bf16[512,2048]{1,0:T(8,128)(2,1)S(1)} %copy-done.5, bf16[2048,10240]{1,0:T(8,128)(2,1)} %b_ref.15), custom_call_target="tpu_custom_call" | custom-call | flops 167772160 | bytes 622592 | tf_op jit(solution)/shard_map/pallas_call | solution.py:45
  47.0 2.1 collective-permute-start.8
  49.0 7.2 %shard_map.89 = f32[512,1280]{1,0:T(8,128)} custom-call(s32[1]{0:T(128)} %bitcast.17.first_ref, bf16[512,2048]{1,0:T(8,128)(2,1)S(1)} %copy-done.5, bf16[2048,10240]{1,0:T(8,128)(2,1)} %b_ref.15), custom_call_target="tpu_custom_call" | custom-call | flops 167772160 | bytes 622592 | tf_op jit(solution)/shard_map/pallas_call | solution.py:45
  56.8 15.0 %fusion.44 = (f32[512]{0:T(512)S(1)}, f32[512,2560]{1,0:T(8,128)}) fusion(bf16[512,3584]{1,0:T(8,128)(2,1)S(1)} %copy-done, bf16[3584,2560]{1,0:T(8,128)(2,1)} %param.9), kind=kOutput, calls=%fused_computation.99 | convolution fusion | flops 9396551680 | bytes 27265024 | tf_op jit(solution)/shard_map/dot_general | solution.py:259
  71.8 6.4 %shard_map.92 = f32[512,1280]{1,0:T(8,128)S(1)} custom-call(s32[1]{0:T(128)} %bitcast.18.first_ref, bf16[512,2048]{1,0:T(8,128)(2,1)S(1)} %copy-done.5, bf16[2048,10240]{1,0:T(8,128)(2,1)} %b_ref.15, f32[512,1280]{1,0:T(8,128)} %collective-permute-done.7.rest_0_), custom_call_target="tpu_custom_call" | custom-call | flops 167772160 | bytes 622592 | tf_op jit(solution)/shard_map/pallas_call | solution.py:45
  78.3 6.5 %shard_map.90 = f32[512,1280]{1,0:T(8,128)S(1)} custom-call(s32[1]{0:T(128)} %bitcast.16.first_ref, bf16[512,2048]{1,0:T(8,128)(2,1)S(1)} %copy-done.5, bf16[2048,10240]{1,0:T(8,128)(2,1)} %b_ref.15, f32[512,1280]{1,0:T(8,128)} %collective-permute-done.5.rest_0_), custom_call_target="tpu_custom_call" | custom-call | flops 167772160 | bytes 622592 | tf_op jit(solution)/shard_map/pallas_call | solution.py:45
  84.8 1.6 convert_add_fusion
  86.5 20.4 %collective-permute-done.6 = f16[512,1280]{1,0:T(8,128)(2,1)} collective-permute-done((f16[512,1280]{1,0:T(8,128)(2,1)S(1)}, f16[512,1280]{1,0:T(8,128)(2,1)}, u32[]{:S(2)}, u32[]{:S(2)}) %collective-permute-start.6) | collective-permute-done | bytes 1310752 | tf_op jit(solution)/shard_map/ppermute | solution.py:21
  106.9 1.8 convert_add_fusion.1
  108.7 4.3 %fusion.42 = (f32[512]{0:T(512)S(1)}, pred[512,2560]{1,0:T(8,128)(4,1)S(1)}) fusion(f32[512,1280]{1,0:T(8,128)S(1)} %convert_add_fusion, f32[512,1280]{1,0:T(8,128)S(1)} %convert_add_fusion.1, s32[512]{0:T(512)S(1)} %copy-done.23, s32[2560]{0:T(1024)S(1)} %iota_add_fusion, s32[2560]{0:T(1024)S(1)} %get-tuple-element.95, s32[2560]{0:T(1024)S(1)} %get-tuple-element.96, ...), kind=kOutput, calls=%fused_computation.97 | convolution fusion | flops 858684928 | bytes 6916096 | tf_op jit(solution)/shard_map/dot_general | solution.py:207
  113.0 4.9 %fusion.4 = (f32[512]{0:T(512)S(1)}, f32[512]{0:T(512)S(1)}, f32[512]{0:T(512)S(1)}, f32[512]{0:T(512)S(1)}) fusion(f32[512,2560]{1,0:T(8,128)S(1)} %bitcast.87, s32[2560]{0:T(1024)S(1)} %iota_add_fusion, s32[512]{0:T(512)S(1)} %copy-done.23, pred[512,2560]{1,0:T(8,128)(4,1)S(1)} %get-tuple-element.92, f32[512,1280]{1,0:T(8,128)S(1)} %convert_add_fusion, ...), kind=kLoop, calls=%fused_computation.7 | loop fusion | flops 19658752 | bytes 11821056 | tf_op jit(solution)/shard_map/reduce_sum | solution.py:281
  117.9 0.6 stack.51.part_ref
  118.6 13.1 %shard_map.93 = f32[8,512]{1,0:T(8,128)} custom-call(f32[8,512]{1,0:T(8,128)} %stack.51.part_ref), custom_call_target="tpu_custom_call" | custom-call | tf_op jit(solution)/shard_map/pallas_call | solution.py:168
  131.6 1.5 fusion.43
  133.2 6.6 %fusion.6.grad_ref = bf16[512,2560]{1,0:T(8,128)(2,1)S(1)} fusion(f32[512,2560]{1,0:T(8,128)} %get-tuple-element.94, pred[512,2560]{1,0:T(8,128)(4,1)} %copy-done.14, f32[512]{0:T(512)S(1)} %bitcast.100, f32[512]{0:T(512)S(1)} %bitcast.96, f32[512]{0:T(512)S(1)} %bitcast.98, f32[512]{0:T(512)S(1)} %bitcast.94, s32[2560]{0:T(1024)S(1)} %iota_add_fusion, ...), kind=kLoop, calls=%fused_computation.9 | loop fusion | flops 19660800 | bytes 14438400 | tf_op jit(solution)/shard_map/convert_element_type | solution.py:302
  139.8 8.1 %fusion.9 = f32[512,1792]{1,0:T(8,128)S(1)} fusion(bf16[512,2560]{1,0:T(8,128)(2,1)S(1)} %fusion.6.grad_ref, bf16[3584,2560]{1,0:T(8,128)(2,1)} %param.9), kind=kOutput, calls=%fused_computation.19 | convolution fusion | flops 4698537984 | bytes 15466496 | tf_op jit(solution)/shard_map/dot_general | solution.py:313
  147.9 8.1 %fusion.12 = f32[512,1792]{1,0:T(8,128)S(1)} fusion(bf16[512,2560]{1,0:T(8,128)(2,1)S(1)} %fusion.6.grad_ref, bf16[3584,2560]{1,0:T(8,128)(2,1)} %param.9), kind=kOutput, calls=%fused_computation.20 | convolution fusion | flops 4698537984 | bytes 15466496 | tf_op jit(solution)/shard_map/dot_general | solution.py:313
  156.0 1.5 constant_dynamic-slice_fusion.2
  157.6 1.5 constant_dynamic-slice_fusion
  159.1 1.1 fusion.17
  160.7 2.0 copy-done.1
  162.7 3.1 %shard_map.94.rest_0_ = bf16[3584,2560]{1,0:T(8,128)(2,1)} custom-call(bf16[512,3584]{1,0:T(8,128)(2,1)S(1)} %copy-done.1, bf16[512,2560]{1,0:T(8,128)(2,1)S(1)} %fusion.6.grad_ref), custom_call_target="tpu_custom_call" | custom-call | flops 1342177280 | bytes 5767168 | tf_op jit(solution)/shard_map/pallas_call | solution.py:72
  165.8 3.1 %shard_map.95.rest_0_ = bf16[3584,2560]{1,0:T(8,128)(2,1)} custom-call(bf16[512,3584]{1,0:T(8,128)(2,1)S(1)} %copy-done.1, bf16[512,2560]{1,0:T(8,128)(2,1)S(1)} %fusion.6.grad_ref, bf16[3584,2560]{1,0:T(8,128)(2,1)} %shard_map.94.rest_0_), custom_call_target="tpu_custom_call", output_to_operand_aliasing={{}: (2, {})} | custom-call | flops 1342177280 | bytes 5767168 | tf_op jit(solution)/shard_map/pallas_call | solution.py:72
  168.9 1.5 bitcast_add_fusion.1
  170.7 1.9 bitcast_add_fusion
  172.6 0.9 fusion.19
  173.5 0.6 collective-permute-start.11
  174.1 1.7 collective-permute-start.12
  175.8 2.0 copy-done.2
  177.9 3.1 %shard_map.96.rest_0_ = bf16[3584,2560]{1,0:T(8,128)(2,1)} custom-call(bf16[512,3584]{1,0:T(8,128)(2,1)S(1)} %copy-done.2, bf16[512,2560]{1,0:T(8,128)(2,1)S(1)} %fusion.6.grad_ref, bf16[3584,2560]{1,0:T(8,128)(2,1)} %shard_map.95.rest_0_), custom_call_target="tpu_custom_call", output_to_operand_aliasing={{}: (2, {})} | custom-call | flops 1342177280 | bytes 5767168 | tf_op jit(solution)/shard_map/pallas_call | solution.py:72
  181.0 3.1 %shard_map.97.rest_0_ = bf16[3584,2560]{1,0:T(8,128)(2,1)} custom-call(bf16[512,3584]{1,0:T(8,128)(2,1)S(1)} %copy-done.2, bf16[512,2560]{1,0:T(8,128)(2,1)S(1)} %fusion.6.grad_ref, bf16[3584,2560]{1,0:T(8,128)(2,1)} %shard_map.96.rest_0_), custom_call_target="tpu_custom_call", output_to_operand_aliasing={{}: (2, {})} | custom-call | flops 1342177280 | bytes 5767168 | tf_op jit(solution)/shard_map/pallas_call | solution.py:72
  184.1 3.1 %shard_map.98.rest_0_ = bf16[3584,2560]{1,0:T(8,128)(2,1)} custom-call(bf16[512,3584]{1,0:T(8,128)(2,1)S(1)} %copy-done.2, bf16[512,2560]{1,0:T(8,128)(2,1)S(1)} %fusion.6.grad_ref, bf16[3584,2560]{1,0:T(8,128)(2,1)} %shard_map.97.rest_0_), custom_call_target="tpu_custom_call", output_to_operand_aliasing={{}: (2, {})} | custom-call | flops 1342177280 | bytes 5767168 | tf_op jit(solution)/shard_map/pallas_call | solution.py:72
  187.1 0.8 copy-done.17
  187.9 1.1 bitcast_add_fusion.3
  189.1 0.7 fusion.23
  189.8 1.1 bitcast_add_fusion.2
  190.9 0.9 copy-done.15
  191.8 0.7 fusion.24
  192.5 0.6 collective-permute-start.13
  193.1 1.3 collective-permute-start.14
  194.4 2.0 copy-done.3
  196.4 3.1 %shard_map.99.rest_0_ = bf16[3584,2560]{1,0:T(8,128)(2,1)} custom-call(bf16[512,3584]{1,0:T(8,128)(2,1)S(1)} %copy-done.3, bf16[512,2560]{1,0:T(8,128)(2,1)S(1)} %fusion.6.grad_ref, bf16[3584,2560]{1,0:T(8,128)(2,1)} %shard_map.98.rest_0_), custom_call_target="tpu_custom_call", output_to_operand_aliasing={{}: (2, {})} | custom-call | flops 1342177280 | bytes 5767168 | tf_op jit(solution)/shard_map/pallas_call | solution.py:72
  200.0 1.0 bitcast_add_fusion.5
  201.0 1.0 bitcast_add_fusion.4
  202.1 1.3 collective-permute-start.15
  203.4 0.8 collective-permute-start.16
  204.2 3.1 %shard_map.100 = bf16[3584,2560]{1,0:T(8,128)(2,1)} custom-call(bf16[512,3584]{1,0:T(8,128)(2,1)S(1)} %copy-done.3, bf16[512,2560]{1,0:T(8,128)(2,1)S(1)} %fusion.6.grad_ref, bf16[3584,2560]{1,0:T(8,128)(2,1)} %shard_map.99.rest_0_), custom_call_target="tpu_custom_call", output_to_operand_aliasing={{}: (2, {})} | custom-call | flops 1342177280 | bytes 5767168 | tf_op jit(solution)/shard_map/pallas_call | solution.py:72
  207.3 1.1 collective-permute-done.16
  208.5 2.5 %collective-permute-start.18 = (f16[16,1792]{1,0:T(8,128)(2,1)S(1)}, f16[16,1792]{1,0:T(8,128)(2,1)S(1)}, u32[]{:S(2)}, u32[]{:S(2)}) collective-permute-start(f16[16,1792]{1,0:T(8,128)(2,1)S(1)} %fusion.28), channel_id=1, source_target_pairs={{0,16},{4,20},{8,24},{12,28},{16,0},{20,4},{24,8},{28,12},{1,17},{... | collective-permute-start | bytes 172040 | tf_op jit(solution)/shard_map/ppermute | solution.py:21
  211.0 0.6 add_reduce_fusion
  212.3 0.6 collective-permute-start.17
  212.9 0.9 collective-permute-done.18
  213.8 3.7 %collective-permute-done.17 = f16[16,1792]{1,0:T(8,128)(2,1)S(1)} collective-permute-done((f16[16,1792]{1,0:T(8,128)(2,1)S(1)}, f16[16,1792]{1,0:T(8,128)(2,1)S(1)}, u32[]{:S(2)}, u32[]{:S(2)}) %collective-permute-start.17) | collective-permute-done | bytes 57376 | tf_op jit(solution)/shard_map/ppermute | solution.py:21
  217.4 0.7 maximum_multiply_fusion
  (87 shorter events, 3.6 us)
Async XLA Ops:
  0.7 1.6 copy-start.4
  2.3 7.7 %copy-start.5 = (bf16[512,2048]{1,0:T(8,128)(2,1)S(1)}, bf16[512,2048]{1,0:T(8,128)(2,1)}, u32[]{:S(2)}) copy-start(bf16[512,2048]{1,0:T(8,128)(2,1)} %a_ref.15) | copy-start | bytes 6291460
  9.5 16.1 %collective-permute-start.3 = (f32[512,1280]{1,0:T(8,128)}, f32[512,1280]{1,0:T(8,128)}, u32[]{:S(2)}, u32[]{:S(2)}) collective-permute-start(f32[512,1280]{1,0:T(8,128)} %shard_map.85), channel_id=1, source_target_pairs={{0,1},{1,0},{2,3},{3,2},{4,5},{5,4},{6,7},{7,6},{8,9},{9,8},{10,11... | collective-permute-start | bytes 7864328 | tf_op jit(solution)/shard_map/ppermute | solution.py:21
  9.9 7.1 %copy-start.18 = (s32[128,640]{1,0:T(8,128)S(1)}, s32[128,640]{1,0:T(8,128)}, u32[]{:S(2)}) copy-start(s32[128,640]{1,0:T(8,128)} %param.10) | copy-start | bytes 983044
  17.0 15.2 %collective-permute-start.4 = (f32[512,1280]{1,0:T(8,128)}, f32[512,1280]{1,0:T(8,128)}, u32[]{:S(2)}, u32[]{:S(2)}) collective-permute-start(f32[512,1280]{1,0:T(8,128)} %shard_map.87), channel_id=1, source_target_pairs={{0,1},{1,0},{2,3},{3,2},{4,5},{5,4},{6,7},{7,6},{8,9},{9,8},{10,11... | collective-permute-start | bytes 7864328 | tf_op jit(solution)/shard_map/ppermute | solution.py:21
  17.3 5.5 %collective-permute-start.2 = (s32[128,160]{0,1:T(8,128)S(1)}, s32[128,160]{0,1:T(8,128)S(1)}, u32[]{:S(2)}, u32[]{:S(2)}) collective-permute-start(s32[128,160]{0,1:T(8,128)S(1)} %get-tuple-element.82), channel_id=1, source_target_pairs={{0,3},{1,2},{2,1},{3,0},{4,7},{5,6},{6,5},{7,4},{8,11},{9,10},{10,... | collective-permute-start | bytes 245768 | tf_op jit(solution)/shard_map/ppermute | solution.py:192
  19.9 4.8 %collective-permute-start.1 = (s32[128,160]{0,1:T(8,128)S(1)}, s32[128,160]{0,1:T(8,128)S(1)}, u32[]{:S(2)}, u32[]{:S(2)}) collective-permute-start(s32[128,160]{0,1:T(8,128)S(1)} %get-tuple-element.83), channel_id=1, source_target_pairs={{0,2},{1,3},{2,0},{3,1},{4,6},{5,7},{6,4},{7,5},{8,10},{9,11},{10,... | collective-permute-start | bytes 245768 | tf_op jit(solution)/shard_map/ppermute | solution.py:192
  20.4 4.4 %collective-permute-start = (s32[128,160]{0,1:T(8,128)S(1)}, s32[128,160]{0,1:T(8,128)S(1)}, u32[]{:S(2)}, u32[]{:S(2)}) collective-permute-start(s32[128,160]{0,1:T(8,128)S(1)} %get-tuple-element.84), channel_id=1, source_target_pairs={{0,1},{1,0},{2,3},{3,2},{4,5},{5,4},{6,7},{7,6},{8,9},{9,8},{10,11... | collective-permute-start | bytes 245768 | tf_op jit(solution)/shard_map/ppermute | solution.py:192
  46.9 24.9 %collective-permute-start.7 = (f32[512,1280]{1,0:T(8,128)}, f32[512,1280]{1,0:T(8,128)}, u32[]{:S(2)}, u32[]{:S(2)}) collective-permute-start(f32[512,1280]{1,0:T(8,128)} %shard_map.91), channel_id=1, source_target_pairs={{0,1},{1,0},{2,3},{3,2},{4,5},{5,4},{6,7},{7,6},{8,9},{9,8},{10,11... | collective-permute-start | bytes 7864328 | tf_op jit(solution)/shard_map/ppermute | solution.py:21
  47.0 37.8 %collective-permute-start.8 = (f16[512,1280]{1,0:T(8,128)(2,1)}, f16[512,1280]{1,0:T(8,128)(2,1)}, u32[]{:S(2)}, u32[]{:S(2)}) collective-permute-start(f16[512,1280]{1,0:T(8,128)(2,1)} %convert_element_type.130), channel_id=1, source_target_pairs={{0,2},{1,3},{2,0},{3,1},{4,6},{5,7},{6,4},{7,5},{8,10},{9,11},{10,... | collective-permute-start | bytes 3932168 | tf_op jit(solution)/shard_map/ppermute | solution.py:21
  49.0 7.8 %copy-start = (bf16[512,3584]{1,0:T(8,128)(2,1)S(1)}, bf16[512,3584]{1,0:T(8,128)(2,1)}, u32[]{:S(2)}) copy-start(bf16[512,3584]{1,0:T(8,128)(2,1)} %hidden_ref.6) | copy-start | bytes 11010052
  56.3 22.0 %collective-permute-start.5 = (f32[512,1280]{1,0:T(8,128)}, f32[512,1280]{1,0:T(8,128)}, u32[]{:S(2)}, u32[]{:S(2)}) collective-permute-start(f32[512,1280]{1,0:T(8,128)} %shard_map.89), channel_id=1, source_target_pairs={{0,1},{1,0},{2,3},{3,2},{4,5},{5,4},{6,7},{7,6},{8,9},{9,8},{10,11... | collective-permute-start | bytes 7864328 | tf_op jit(solution)/shard_map/ppermute | solution.py:21
  56.5 50.4 %collective-permute-start.6 = (f16[512,1280]{1,0:T(8,128)(2,1)S(1)}, f16[512,1280]{1,0:T(8,128)(2,1)}, u32[]{:S(2)}, u32[]{:S(2)}) collective-permute-start(f16[512,1280]{1,0:T(8,128)(2,1)S(1)} %convert_element_type.129), channel_id=1, source_target_pairs={{0,2},{1,3},{2,0},{3,1},{4,6},{5,7},{6,4},{7,5},{8,10},{9,11},{10,... | collective-permute-start | bytes 3932168 | tf_op jit(solution)/shard_map/ppermute | solution.py:21
  86.4 26.6 %copy-start.6 = (f32[512,1280]{1,0:T(8,128)}, f32[512,1280]{1,0:T(8,128)S(1)}, u32[]{:S(2)}) copy-start(f32[512,1280]{1,0:T(8,128)S(1)} %convert_add_fusion) | copy-start | bytes 7864324
  86.4 22.3 %copy-start.19 = (bf16[512,160]{0,1:T(8,128)(2,1)S(1)}, bf16[512,160]{0,1:T(8,128)(2,1)}, u32[]{:S(2)}) copy-start(bf16[512,160]{0,1:T(8,128)(2,1)} %get-tuple-element.75) | copy-start | bytes 491524
  86.4 22.3 %copy-start.20 = (bf16[512,160]{0,1:T(8,128)(2,1)S(1)}, bf16[512,160]{0,1:T(8,128)(2,1)}, u32[]{:S(2)}) copy-start(bf16[512,160]{0,1:T(8,128)(2,1)} %get-tuple-element.76) | copy-start | bytes 491524
  86.4 22.3 %copy-start.23 = (s32[512]{0:T(512)S(1)}, s32[512]{0:T(512)}, u32[]{:S(2)}) copy-start(s32[512]{0:T(512)} %param.11) | copy-start | bytes 6148
  106.9 6.1 %slice-start = ((s8[5242880]{0:T(1024)(128)(4,1)}), s8[4194304]{0:T(1024)(128)(4,1)S(1)}, s32[]{:S(2)}) async-start(s8[5242880]{0:T(1024)(128)(4,1)} %bitcast.86), calls=%async_computation | async-start | bytes 8388608
  108.7 4.3 %copy-start.7 = (f32[512,1280]{1,0:T(8,128)}, f32[512,1280]{1,0:T(8,128)S(1)}, u32[]{:S(2)}) copy-start(f32[512,1280]{1,0:T(8,128)S(1)} %convert_add_fusion.1) | copy-start | bytes 7864324
  108.7 4.3 %slice-start.1 = ((s8[5242880]{0:T(1024)(128)(4,1)}), s8[1048576]{0:T(1024)(128)(4,1)S(1)}, s32[]{:S(2)}) async-start(s8[5242880]{0:T(1024)(128)(4,1)} %bitcast.86), calls=%async_computation.1 | async-start | bytes 2097152
  113.0 4.9 %copy-start.14 = (pred[512,2560]{1,0:T(8,128)(4,1)}, pred[512,2560]{1,0:T(8,128)(4,1)S(1)}, u32[]{:S(2)}) copy-start(pred[512,2560]{1,0:T(8,128)(4,1)S(1)} %get-tuple-element.92) | copy-start | bytes 3932164
  160.2 8.7 %collective-permute-start.9 = (f16[2,2,2,2,16,1792]{5,4,0,1,2,3:T(8,128)(2,1)S(1)}, f16[2,2,2,2,16,1792]{5,4,0,1,2,3:T(8,128)(2,1)}, u32[]{:S(2)}, u32[]{:S(2)}) collective-permute-start(f16[2,2,2,2,16,1792]{5,4,0,1,2,3:T(8,128)(2,1)S(1)} %fusion.16), channel_id=1, source_target_pairs={{0,1},{1,0},{2,3},{3,2},{4,5},{5,4},{6,7},{7,6},{8,9},{9,8},{10,11... | collective-permute-start | bytes 2752520 | tf_op jit(solution)/shard_map/ppermute | solution.py:21
  160.2 8.7 %collective-permute-start.10 = (f16[2,2,2,2,16,1792]{5,4,0,1,3,2:T(8,128)(2,1)}, f16[2,2,2,2,16,1792]{5,4,0,1,3,2:T(8,128)(2,1)}, u32[]{:S(2)}, u32[]{:S(2)}) collective-permute-start(f16[2,2,2,2,16,1792]{5,4,0,1,3,2:T(8,128)(2,1)} %fusion.17), channel_id=1, source_target_pairs={{0,1},{1,0},{2,3},{3,2},{4,5},{5,4},{6,7},{7,6},{8,9},{9,8},{10,11... | collective-permute-start | bytes 2752520 | tf_op jit(solution)/shard_map/ppermute | solution.py:21
  160.7 2.0 copy-start.1
  165.8 3.1 %copy-start.12 = (f32[2,2,2,2,1,16,1792]{6,5,4,3,2,1,0:T(8,128)S(1)}, f32[2,2,2,2,1,16,1792]{6,5,4,3,2,1,0:T(8,128)}, u32[]{:S(2)}) copy-start(f32[2,2,2,2,1,16,1792]{6,5,4,3,2,1,0:T(8,128)} %get-tuple-element.74) | copy-start | bytes 5505028
  168.9 1.8 copy-start.13
  170.4 3.0 %copy-start.8 = (f32[2,2,2,2,16,1792]{5,4,0,1,2,3:T(8,128)}, f32[2,2,2,2,16,1792]{5,4,0,1,2,3:T(8,128)S(1)}, u32[]{:S(2)}) copy-start(f32[2,2,2,2,16,1792]{5,4,0,1,2,3:T(8,128)S(1)} %bitcast_add_fusion.1) | copy-start | bytes 5505028
  172.6 1.6 copy-start.10
  173.5 13.7 %collective-permute-start.11 = (f16[2,2,2,16,1792]{4,3,0,1,2:T(8,128)(2,1)S(1)}, f16[2,2,2,16,1792]{4,3,0,1,2:T(8,128)(2,1)S(1)}, u32[]{:S(2)}, u32[]{:S(2)}) collective-permute-start(f16[2,2,2,16,1792]{4,3,0,1,2:T(8,128)(2,1)S(1)} %fusion.18), channel_id=1, source_target_pairs={{0,2},{1,3},{2,0},{3,1},{4,6},{5,7},{6,4},{7,5},{8,10},{9,11},{10,... | collective-permute-start | bytes 1376264 | tf_op jit(solution)/shard_map/ppermute | solution.py:21
  174.1 13.8 %collective-permute-start.12 = (f16[2,2,2,16,1792]{4,3,0,1,2:T(8,128)(2,1)}, f16[2,2,2,16,1792]{4,3,0,1,2:T(8,128)(2,1)}, u32[]{:S(2)}, u32[]{:S(2)}) collective-permute-start(f16[2,2,2,16,1792]{4,3,0,1,2:T(8,128)(2,1)} %fusion.19), channel_id=1, source_target_pairs={{0,4},{4,0},{8,12},{12,8},{16,20},{20,16},{24,28},{28,24},{1,5},{5... | collective-permute-start | bytes 1376264 | tf_op jit(solution)/shard_map/ppermute | solution.py:21
  175.8 2.0 copy-start.2
  184.0 3.9 %copy-start.9 = (f32[2,2,2,2,16,1792]{5,4,0,1,2,3:T(8,128)S(1)}, f32[2,2,2,2,16,1792]{5,4,0,1,2,3:T(8,128)}, u32[]{:S(2)}) copy-start(f32[2,2,2,2,16,1792]{5,4,0,1,2,3:T(8,128)} %copy-done.8) | copy-start | bytes 5505028
  184.1 5.7 %copy-start.11 = (f32[2,2,2,2,16,1792]{5,4,0,1,3,2:T(8,128)S(1)}, f32[2,2,2,2,16,1792]{5,4,0,1,3,2:T(8,128)}, u32[]{:S(2)}) copy-start(f32[2,2,2,2,16,1792]{5,4,0,1,3,2:T(8,128)} %copy-done.10) | copy-start | bytes 5505028
  187.1 0.8 copy-start.17
  190.9 0.9 copy-start.15
  192.5 7.5 %collective-permute-start.13 = (f16[2,2,16,1792]{3,2,0,1:T(8,128)(2,1)}, f16[2,2,16,1792]{3,2,0,1:T(8,128)(2,1)}, u32[]{:S(2)}, u32[]{:S(2)}) collective-permute-start(f16[2,2,16,1792]{3,2,0,1:T(8,128)(2,1)} %fusion.23), channel_id=1, source_target_pairs={{0,4},{4,0},{8,12},{12,8},{16,20},{20,16},{24,28},{28,24},{1,5},{5... | collective-permute-start | bytes 688136 | tf_op jit(solution)/shard_map/ppermute | solution.py:21
  193.1 6.9 %collective-permute-start.14 = (f16[2,2,16,1792]{3,2,0,1:T(8,128)(2,1)}, f16[2,2,16,1792]{3,2,0,1:T(8,128)(2,1)}, u32[]{:S(2)}, u32[]{:S(2)}) collective-permute-start(f16[2,2,16,1792]{3,2,0,1:T(8,128)(2,1)} %fusion.24), channel_id=1, source_target_pairs={{0,2},{1,3},{2,0},{3,1},{4,6},{5,7},{6,4},{7,5},{8,10},{9,11},{10,... | collective-permute-start | bytes 688136 | tf_op jit(solution)/shard_map/ppermute | solution.py:21
  194.4 2.0 copy-start.3
  196.4 4.6 %copy-start.16 = (f32[2,2,2,16,1792]{4,3,0,1,2:T(8,128)S(1)}, f32[2,2,2,16,1792]{4,3,0,1,2:T(8,128)}, u32[]{:S(2)}) copy-start(f32[2,2,2,16,1792]{4,3,0,1,2:T(8,128)} %copy-done.15) | copy-start | bytes 2752516
  202.1 8.9 %copy-start.21 = (f32[1,512]{1,0:T(1,128)S(1)}, f32[1,512]{1,0:T(1,128)}, u32[]{:S(2)}) copy-start(f32[1,512]{1,0:T(1,128)} %get-tuple-element.85) | copy-start | bytes 6148
  202.1 8.9 %copy-start.22 = (f32[1,512]{1,0:T(1,128)S(1)}, f32[1,512]{1,0:T(1,128)}, u32[]{:S(2)}) copy-start(f32[1,512]{1,0:T(1,128)} %get-tuple-element.88) | copy-start | bytes 6148
  202.1 5.2 %collective-permute-start.15 = (f16[2,16,1792]{2,1,0:T(8,128)(2,1)S(1)}, f16[2,16,1792]{2,1,0:T(8,128)(2,1)S(1)}, u32[]{:S(2)}, u32[]{:S(2)}) collective-permute-start(f16[2,16,1792]{2,1,0:T(8,128)(2,1)S(1)} %fusion.25), channel_id=1, source_target_pairs={{0,8},{4,12},{8,0},{12,4},{16,24},{20,28},{24,16},{28,20},{1,9},{5... | collective-permute-start | bytes 344072 | tf_op jit(solution)/shard_map/ppermute | solution.py:21
  203.4 5.0 %collective-permute-start.16 = (f16[2,16,1792]{2,1,0:T(8,128)(2,1)S(1)}, f16[2,16,1792]{2,1,0:T(8,128)(2,1)S(1)}, u32[]{:S(2)}, u32[]{:S(2)}) collective-permute-start(f16[2,16,1792]{2,1,0:T(8,128)(2,1)S(1)} %fusion.26), channel_id=1, source_target_pairs={{0,8},{4,12},{8,0},{12,4},{16,24},{20,28},{24,16},{28,20},{1,9},{5... | collective-permute-start | bytes 344072 | tf_op jit(solution)/shard_map/ppermute | solution.py:21
  208.5 5.2 %collective-permute-start.18 = (f16[16,1792]{1,0:T(8,128)(2,1)S(1)}, f16[16,1792]{1,0:T(8,128)(2,1)S(1)}, u32[]{:S(2)}, u32[]{:S(2)}) collective-permute-start(f16[16,1792]{1,0:T(8,128)(2,1)S(1)} %fusion.28), channel_id=1, source_target_pairs={{0,16},{4,20},{8,24},{12,28},{16,0},{20,4},{24,8},{28,12},{1,17},{... | collective-permute-start | bytes 172040 | tf_op jit(solution)/shard_map/ppermute | solution.py:21
  212.3 5.1 %collective-permute-start.17 = (f16[16,1792]{1,0:T(8,128)(2,1)S(1)}, f16[16,1792]{1,0:T(8,128)(2,1)S(1)}, u32[]{:S(2)}, u32[]{:S(2)}) collective-permute-start(f16[16,1792]{1,0:T(8,128)(2,1)S(1)} %fusion.27), channel_id=1, source_target_pairs={{0,16},{4,20},{8,24},{12,28},{16,0},{20,4},{24,8},{28,12},{1,17},{... | collective-permute-start | bytes 172040 | tf_op jit(solution)/shard_map/ppermute | solution.py:21

commit v3 on v2

--- a/solution.py
+++ b/solution.py
@@ -249,7 +249,9 @@
     sent = []
     for at, lower in enumerate((0, half)):
         away = product(mine ^ 2, lower, jnp.float32, (far[at],)).astype(jnp.float16)
-        away, mine, student_hidden = lax.optimization_barrier((away, mine, student_hidden))
+        away, mine, student_hidden, grammar_bits = lax.optimization_barrier(
+            (away, mine, student_hidden, grammar_bits)
+        )
         sent.append(swapped(away, "tok", 1))
     for lower in (0, half):
         away = product(mine ^ 1, lower, jnp.float32)

time: 221 us -> 216 us (0.977)
  waiting for transfers between devices: 31 us -> 25.4 us
    ppermute x3, waiting for transfers between devices: 4.33 us -> 0.01 us  [words_here(): lax.ppermute(piece, 'tok', [(i, i ^ step) for i in range(groups)])]
    unnamed x53 -> x50, local copies, waits for them, and re-layouts: 9.82 us -> 9.63 us
  transfers between devices with their start and end apart: 19 -> 19, of which waited for: 7 -> 5; matrix products, arithmetic and copies ran while one was open for 8% -> 9% of each run, Pallas kernels for 25% -> 29%
where the time goes in v3:
time: 216 us; the launch traced here: 215 us
  Pallas kernels  88.8 us (41%)
  matrix products  35.6 us (16%)
  other arithmetic  30.9 us (14%)
  waiting for transfers between devices  25.4 us (12%)
  starting transfers between devices  15.8 us (7%)
  local copies, waits for them, and re-layouts  15.7 us (7%)
  between operations  2.89 us (1%)
    pallas_call x8, Pallas kernels, chunk_product(): pl.pallas_call(chunk_kernel, grid_spec=grid_spec, out_shape=jax.ShapeDtyp...  54.3 us
    ppermute x16, waiting for transfers between devices, swapped(): return lax.ppermute(value, axis, [(i, i ^ 1 << bit) for i in range(size)])  25.4 us
    pallas_call x7, Pallas kernels, grad_rows(): pl.pallas_call(grad_kernel, grid=(cut,), in_specs=[pl.BlockSpec((tokens,...  21.6 us
    dot_general x2, matrix products, per_device(): lax.dot_general(logit_grad, lax.slice_in_dim(student_head, at * width, (a...  16.3 us
    dot_general x1, matrix products, per_device(): jnp.dot(student_hidden, student_head, preferred_element_type=jnp.float32)  15 us
    pallas_call x1, Pallas kernels, merged_stats(): pl.pallas_call(functools.partial(stats_kernel, groups, ways), out_shape=j...  12.9 us
    ppermute x16, starting transfers between devices, swapped(): return lax.ppermute(value, axis, [(i, i ^ 1 << bit) for i in range(size)])  12.7 us
    unnamed x50, local copies, waits for them, and re-layouts  9.63 us
  transfers between devices with their start and end apart: 19, of which 5 were waited for; matrix products, arithmetic and copies ran while one was open for 9% of the time, Pallas kernels for 29%

profile of v3, /device:TPU:0, one launch (start us, length us, event | category | flops | bytes accessed | tf_op | source)
XLA Modules:
  0.0 215.0 jit_solution(17495266598983542226)
XLA Ops:
  0.7 1.6 copy-done.4
  2.3 7.2 %shard_map.85 = f32[512,1280]{1,0:T(8,128)} custom-call(s32[1]{0:T(128)} %bitcast.1.first_ref, bf16[512,2048]{1,0:T(8,128)(2,1)S(1)} %copy-done.4, bf16[2048,10240]{1,0:T(8,128)(2,1)} %b_ref.15), custom_call_target="tpu_custom_call" | custom-call | flops 167772160 | bytes 622592 | tf_op jit(solution)/shard_map/pallas_call | solution.py:45
  9.9 7.0 %shard_map.87 = f32[512,1280]{1,0:T(8,128)} custom-call(s32[1]{0:T(128)} %bitcast.3.first_ref, bf16[512,2048]{1,0:T(8,128)(2,1)S(1)} %copy-done.5, bf16[2048,10240]{1,0:T(8,128)(2,1)} %b_ref.15), custom_call_target="tpu_custom_call" | custom-call | flops 167772160 | bytes 622592 | tf_op jit(solution)/shard_map/pallas_call | solution.py:45
  17.0 6.4 %shard_map.86 = f32[512,1280]{1,0:T(8,128)S(1)} custom-call(s32[1]{0:T(128)} %bitcast.first_ref, bf16[512,2048]{1,0:T(8,128)(2,1)S(1)} %copy-done.5, bf16[2048,10240]{1,0:T(8,128)(2,1)} %b_ref.15, f32[512,1280]{1,0:T(8,128)} %collective-permute-done.rest_0_), custom_call_target="tpu_custom_call" | custom-call | flops 167772160 | bytes 622592 | tf_op jit(solution)/shard_map/pallas_call | solution.py:45
  23.5 1.2 convert_element_type.125
  24.6 6.4 %shard_map.88 = f32[512,1280]{1,0:T(8,128)S(1)} custom-call(s32[1]{0:T(128)} %bitcast.2.first_ref, bf16[512,2048]{1,0:T(8,128)(2,1)S(1)} %copy-done.5, bf16[2048,10240]{1,0:T(8,128)(2,1)} %b_ref.15, f32[512,1280]{1,0:T(8,128)} %collective-permute-done.1.rest_0_), custom_call_target="tpu_custom_call" | custom-call | flops 167772160 | bytes 622592 | tf_op jit(solution)/shard_map/pallas_call | solution.py:45
  31.1 1.2 convert_element_type.126
  32.4 0.7 dynamic-slice_bitcast_fusion.7
  33.1 2.6 %collective-permute-start.4 = (s32[128,160]{0,1:T(8,128)}, s32[128,160]{0,1:T(8,128)}, u32[]{:S(2)}, u32[]{:S(2)}) collective-permute-start(s32[128,160]{0,1:T(8,128)} %get-tuple-element.86), channel_id=1, source_target_pairs={{0,3},{1,2},{2,1},{3,0},{4,7},{5,6},{6,5},{7,4},{8,11},{9,10},{10,... | collective-permute-start | bytes 245768 | tf_op jit(solution)/shard_map/ppermute | solution.py:192
  36.1 7.1 %shard_map.91 = f32[512,1280]{1,0:T(8,128)} custom-call(s32[1]{0:T(128)} %bitcast.19.first_ref, bf16[512,2048]{1,0:T(8,128)(2,1)S(1)} %copy-done.5, bf16[2048,10240]{1,0:T(8,128)(2,1)} %b_ref.15), custom_call_target="tpu_custom_call" | custom-call | flops 167772160 | bytes 622592 | tf_op jit(solution)/shard_map/pallas_call | solution.py:45
  43.3 1.7 collective-permute-start.8
  45.0 7.3 %shard_map.89 = f32[512,1280]{1,0:T(8,128)} custom-call(s32[1]{0:T(128)} %bitcast.17.first_ref, bf16[512,2048]{1,0:T(8,128)(2,1)S(1)} %copy-done.5, bf16[2048,10240]{1,0:T(8,128)(2,1)} %b_ref.15), custom_call_target="tpu_custom_call" | custom-call | flops 167772160 | bytes 622592 | tf_op jit(solution)/shard_map/pallas_call | solution.py:45
  52.9 15.0 %fusion.44 = (f32[512]{0:T(512)S(1)}, f32[512,2560]{1,0:T(8,128)}) fusion(bf16[512,3584]{1,0:T(8,128)(2,1)S(1)} %copy-done, bf16[3584,2560]{1,0:T(8,128)(2,1)} %param.9), kind=kOutput, calls=%fused_computation.99 | convolution fusion | flops 9396551680 | bytes 27265024 | tf_op jit(solution)/shard_map/dot_general | solution.py:261
  67.9 1.0 pad_add_fusion
  69.1 6.4 %shard_map.92 = f32[512,1280]{1,0:T(8,128)S(1)} custom-call(s32[1]{0:T(128)} %bitcast.18.first_ref, bf16[512,2048]{1,0:T(8,128)(2,1)S(1)} %copy-done.5, bf16[2048,10240]{1,0:T(8,128)(2,1)} %b_ref.15, f32[512,1280]{1,0:T(8,128)} %collective-permute-done.7.rest_0_), custom_call_target="tpu_custom_call" | custom-call | flops 167772160 | bytes 622592 | tf_op jit(solution)/shard_map/pallas_call | solution.py:45
  75.5 6.4 %shard_map.90 = f32[512,1280]{1,0:T(8,128)S(1)} custom-call(s32[1]{0:T(128)} %bitcast.16.first_ref, bf16[512,2048]{1,0:T(8,128)(2,1)S(1)} %copy-done.5, bf16[2048,10240]{1,0:T(8,128)(2,1)} %b_ref.15, f32[512,1280]{1,0:T(8,128)} %collective-permute-done.5.rest_0_), custom_call_target="tpu_custom_call" | custom-call | flops 167772160 | bytes 622592 | tf_op jit(solution)/shard_map/pallas_call | solution.py:45
  81.9 1.6 convert_add_fusion
  83.6 19.2 %collective-permute-done.6 = f16[512,1280]{1,0:T(8,128)(2,1)} collective-permute-done((f16[512,1280]{1,0:T(8,128)(2,1)S(1)}, f16[512,1280]{1,0:T(8,128)(2,1)}, u32[]{:S(2)}, u32[]{:S(2)}) %collective-permute-start.6) | collective-permute-done | bytes 1310752 | tf_op jit(solution)/shard_map/ppermute | solution.py:21
  102.8 1.8 convert_add_fusion.1
  104.6 4.3 %fusion.42 = (f32[512]{0:T(512)S(1)}, pred[512,2560]{1,0:T(8,128)(4,1)S(1)}) fusion(f32[512,1280]{1,0:T(8,128)S(1)} %convert_add_fusion, f32[512,1280]{1,0:T(8,128)S(1)} %convert_add_fusion.1, s32[512]{0:T(512)S(1)} %copy-done.22, s32[2560]{0:T(1024)S(1)} %iota_add_fusion, s32[2560]{0:T(1024)S(1)} %get-tuple-element.99, s32[2560]{0:T(1024)S(1)} %get-tuple-element.100, ...), kind=kOutput, calls=%fused_computation.97 | convolution fusion | flops 858684928 | bytes 6916096 | tf_op jit(solution)/shard_map/dot_general | solution.py:207
  108.9 4.9 %fusion.4 = (f32[512]{0:T(512)S(1)}, f32[512]{0:T(512)S(1)}, f32[512]{0:T(512)S(1)}, f32[512]{0:T(512)S(1)}) fusion(f32[512,2560]{1,0:T(8,128)S(1)} %bitcast.87, s32[2560]{0:T(1024)S(1)} %iota_add_fusion, s32[512]{0:T(512)S(1)} %copy-done.22, pred[512,2560]{1,0:T(8,128)(4,1)S(1)} %get-tuple-element.96, f32[512,1280]{1,0:T(8,128)S(1)} %convert_add_fusion, ...), kind=kLoop, calls=%fused_computation.7 | loop fusion | flops 19658752 | bytes 11821056 | tf_op jit(solution)/shard_map/reduce_sum | solution.py:283
  113.8 0.6 stack.51.part_ref
  114.5 12.9 %shard_map.93 = f32[8,512]{1,0:T(8,128)} custom-call(f32[8,512]{1,0:T(8,128)} %stack.51.part_ref), custom_call_target="tpu_custom_call" | custom-call | tf_op jit(solution)/shard_map/pallas_call | solution.py:168
  127.4 1.5 fusion.43
  128.9 6.6 %fusion.6.grad_ref = bf16[512,2560]{1,0:T(8,128)(2,1)S(1)} fusion(f32[512,2560]{1,0:T(8,128)} %get-tuple-element.98, pred[512,2560]{1,0:T(8,128)(4,1)} %copy-done.14, f32[512]{0:T(512)S(1)} %bitcast.97, f32[512]{0:T(512)S(1)} %bitcast.93, f32[512]{0:T(512)S(1)} %bitcast.95, f32[512]{0:T(512)S(1)} %bitcast.91, s32[2560]{0:T(1024)S(1)} %iota_add_fusion, ...), kind=kLoop, calls=%fused_computation.9 | loop fusion | flops 19660800 | bytes 14438400 | tf_op jit(solution)/shard_map/convert_element_type | solution.py:304
  135.5 8.1 %fusion.9 = f32[512,1792]{1,0:T(8,128)S(1)} fusion(bf16[512,2560]{1,0:T(8,128)(2,1)S(1)} %fusion.6.grad_ref, bf16[3584,2560]{1,0:T(8,128)(2,1)} %param.9), kind=kOutput, calls=%fused_computation.19 | convolution fusion | flops 4698537984 | bytes 15466496 | tf_op jit(solution)/shard_map/dot_general | solution.py:315
  143.6 8.1 %fusion.12 = f32[512,1792]{1,0:T(8,128)S(1)} fusion(bf16[512,2560]{1,0:T(8,128)(2,1)S(1)} %fusion.6.grad_ref, bf16[3584,2560]{1,0:T(8,128)(2,1)} %param.9), kind=kOutput, calls=%fused_computation.20 | convolution fusion | flops 4698537984 | bytes 15466496 | tf_op jit(solution)/shard_map/dot_general | solution.py:315
  151.8 1.5 constant_dynamic-slice_fusion.2
  153.4 1.5 constant_dynamic-slice_fusion
  154.9 1.1 fusion.17
  156.4 2.0 copy-done.1
  158.5 3.1 %shard_map.94.rest_0_ = bf16[3584,2560]{1,0:T(8,128)(2,1)} custom-call(bf16[512,3584]{1,0:T(8,128)(2,1)S(1)} %copy-done.1, bf16[512,2560]{1,0:T(8,128)(2,1)S(1)} %fusion.6.grad_ref), custom_call_target="tpu_custom_call" | custom-call | flops 1342177280 | bytes 5767168 | tf_op jit(solution)/shard_map/pallas_call | solution.py:72
  161.5 3.1 %shard_map.95.rest_0_ = bf16[3584,2560]{1,0:T(8,128)(2,1)} custom-call(bf16[512,3584]{1,0:T(8,128)(2,1)S(1)} %copy-done.1, bf16[512,2560]{1,0:T(8,128)(2,1)S(1)} %fusion.6.grad_ref, bf16[3584,2560]{1,0:T(8,128)(2,1)} %shard_map.94.rest_0_), custom_call_target="tpu_custom_call", output_to_operand_aliasing={{}: (2, {})} | custom-call | flops 1342177280 | bytes 5767168 | tf_op jit(solution)/shard_map/pallas_call | solution.py:72
  164.7 1.5 bitcast_add_fusion.1
  166.4 1.9 bitcast_add_fusion
  168.3 0.9 fusion.19
  169.2 0.6 collective-permute-start.11
  169.8 1.7 collective-permute-start.12
  171.6 2.0 copy-done.2
  173.6 3.1 %shard_map.96.rest_0_ = bf16[3584,2560]{1,0:T(8,128)(2,1)} custom-call(bf16[512,3584]{1,0:T(8,128)(2,1)S(1)} %copy-done.2, bf16[512,2560]{1,0:T(8,128)(2,1)S(1)} %fusion.6.grad_ref, bf16[3584,2560]{1,0:T(8,128)(2,1)} %shard_map.95.rest_0_), custom_call_target="tpu_custom_call", output_to_operand_aliasing={{}: (2, {})} | custom-call | flops 1342177280 | bytes 5767168 | tf_op jit(solution)/shard_map/pallas_call | solution.py:72
  176.7 3.1 %shard_map.97.rest_0_ = bf16[3584,2560]{1,0:T(8,128)(2,1)} custom-call(bf16[512,3584]{1,0:T(8,128)(2,1)S(1)} %copy-done.2, bf16[512,2560]{1,0:T(8,128)(2,1)S(1)} %fusion.6.grad_ref, bf16[3584,2560]{1,0:T(8,128)(2,1)} %shard_map.96.rest_0_), custom_call_target="tpu_custom_call", output_to_operand_aliasing={{}: (2, {})} | custom-call | flops 1342177280 | bytes 5767168 | tf_op jit(solution)/shard_map/pallas_call | solution.py:72
  179.8 3.1 %shard_map.98.rest_0_ = bf16[3584,2560]{1,0:T(8,128)(2,1)} custom-call(bf16[512,3584]{1,0:T(8,128)(2,1)S(1)} %copy-done.2, bf16[512,2560]{1,0:T(8,128)(2,1)S(1)} %fusion.6.grad_ref, bf16[3584,2560]{1,0:T(8,128)(2,1)} %shard_map.97.rest_0_), custom_call_target="tpu_custom_call", output_to_operand_aliasing={{}: (2, {})} | custom-call | flops 1342177280 | bytes 5767168 | tf_op jit(solution)/shard_map/pallas_call | solution.py:72
  182.9 0.8 copy-done.18
  183.6 1.1 bitcast_add_fusion.3
  184.7 0.7 fusion.23
  185.5 1.1 bitcast_add_fusion.2
  186.6 0.9 copy-done.15
  187.5 0.7 fusion.24
  188.3 0.6 collective-permute-start.13
  188.9 1.2 collective-permute-start.14
  190.1 2.0 copy-done.3
  192.2 3.1 %shard_map.99.rest_0_ = bf16[3584,2560]{1,0:T(8,128)(2,1)} custom-call(bf16[512,3584]{1,0:T(8,128)(2,1)S(1)} %copy-done.3, bf16[512,2560]{1,0:T(8,128)(2,1)S(1)} %fusion.6.grad_ref, bf16[3584,2560]{1,0:T(8,128)(2,1)} %shard_map.98.rest_0_), custom_call_target="tpu_custom_call", output_to_operand_aliasing={{}: (2, {})} | custom-call | flops 1342177280 | bytes 5767168 | tf_op jit(solution)/shard_map/pallas_call | solution.py:72
  195.8 1.0 bitcast_add_fusion.5
  196.8 1.0 bitcast_add_fusion.4
  197.9 1.3 collective-permute-start.15
  199.2 0.8 collective-permute-start.16
  200.0 3.1 %shard_map.100 = bf16[3584,2560]{1,0:T(8,128)(2,1)} custom-call(bf16[512,3584]{1,0:T(8,128)(2,1)S(1)} %copy-done.3, bf16[512,2560]{1,0:T(8,128)(2,1)S(1)} %fusion.6.grad_ref, bf16[3584,2560]{1,0:T(8,128)(2,1)} %shard_map.99.rest_0_), custom_call_target="tpu_custom_call", output_to_operand_aliasing={{}: (2, {})} | custom-call | flops 1342177280 | bytes 5767168 | tf_op jit(solution)/shard_map/pallas_call | solution.py:72
  203.0 1.2 collective-permute-done.16
  204.4 2.4 %collective-permute-start.18 = (f16[16,1792]{1,0:T(8,128)(2,1)S(1)}, f16[16,1792]{1,0:T(8,128)(2,1)S(1)}, u32[]{:S(2)}, u32[]{:S(2)}) collective-permute-start(f16[16,1792]{1,0:T(8,128)(2,1)S(1)} %fusion.28), channel_id=1, source_target_pairs={{0,16},{4,20},{8,24},{12,28},{16,0},{20,4},{24,8},{28,12},{1,17},{... | collective-permute-start | bytes 172040 | tf_op jit(solution)/shard_map/ppermute | solution.py:21
  206.8 0.6 add_reduce_fusion
  208.0 0.6 collective-permute-start.17
  208.7 1.0 collective-permute-done.18
  209.7 3.5 %collective-permute-done.17 = f16[16,1792]{1,0:T(8,128)(2,1)S(1)} collective-permute-done((f16[16,1792]{1,0:T(8,128)(2,1)S(1)}, f16[16,1792]{1,0:T(8,128)(2,1)S(1)}, u32[]{:S(2)}, u32[]{:S(2)}) %collective-permute-start.17) | collective-permute-done | bytes 57376 | tf_op jit(solution)/shard_map/ppermute | solution.py:21
  213.2 0.7 maximum_multiply_fusion
  (85 shorter events, 3.5 us)
Async XLA Ops:
  0.7 1.6 copy-start.4
  2.3 7.7 %copy-start.5 = (bf16[512,2048]{1,0:T(8,128)(2,1)S(1)}, bf16[512,2048]{1,0:T(8,128)(2,1)}, u32[]{:S(2)}) copy-start(bf16[512,2048]{1,0:T(8,128)(2,1)} %a_ref.15) | copy-start | bytes 6291460
  9.5 7.6 %collective-permute-start = (f32[512,1280]{1,0:T(8,128)}, f32[512,1280]{1,0:T(8,128)}, u32[]{:S(2)}, u32[]{:S(2)}) collective-permute-start(f32[512,1280]{1,0:T(8,128)} %shard_map.85), channel_id=1, source_target_pairs={{0,1},{1,0},{2,3},{3,2},{4,5},{5,4},{6,7},{7,6},{8,9},{9,8},{10,11... | collective-permute-start | bytes 7864328 | tf_op jit(solution)/shard_map/ppermute | solution.py:21
  17.0 7.7 %collective-permute-start.1 = (f32[512,1280]{1,0:T(8,128)}, f32[512,1280]{1,0:T(8,128)}, u32[]{:S(2)}, u32[]{:S(2)}) collective-permute-start(f32[512,1280]{1,0:T(8,128)} %shard_map.87), channel_id=1, source_target_pairs={{0,1},{1,0},{2,3},{3,2},{4,5},{5,4},{6,7},{7,6},{8,9},{9,8},{10,11... | collective-permute-start | bytes 7864328 | tf_op jit(solution)/shard_map/ppermute | solution.py:21
  31.1 1.2 copy-start.19
  33.1 19.2 %collective-permute-start.4 = (s32[128,160]{0,1:T(8,128)}, s32[128,160]{0,1:T(8,128)}, u32[]{:S(2)}, u32[]{:S(2)}) collective-permute-start(s32[128,160]{0,1:T(8,128)} %get-tuple-element.86), channel_id=1, source_target_pairs={{0,3},{1,2},{2,1},{3,0},{4,7},{5,6},{6,5},{7,4},{8,11},{9,10},{10,... | collective-permute-start | bytes 245768 | tf_op jit(solution)/shard_map/ppermute | solution.py:192
  35.7 17.1 %collective-permute-start.3 = (s32[128,160]{0,1:T(8,128)}, s32[128,160]{0,1:T(8,128)}, u32[]{:S(2)}, u32[]{:S(2)}) collective-permute-start(s32[128,160]{0,1:T(8,128)} %get-tuple-element.87), channel_id=1, source_target_pairs={{0,2},{1,3},{2,0},{3,1},{4,6},{5,7},{6,4},{7,5},{8,10},{9,11},{10,... | collective-permute-start | bytes 245768 | tf_op jit(solution)/shard_map/ppermute | solution.py:192
  43.2 25.9 %collective-permute-start.7 = (f32[512,1280]{1,0:T(8,128)}, f32[512,1280]{1,0:T(8,128)}, u32[]{:S(2)}, u32[]{:S(2)}) collective-permute-start(f32[512,1280]{1,0:T(8,128)} %shard_map.91), channel_id=1, source_target_pairs={{0,1},{1,0},{2,3},{3,2},{4,5},{5,4},{6,7},{7,6},{8,9},{9,8},{10,11... | collective-permute-start | bytes 7864328 | tf_op jit(solution)/shard_map/ppermute | solution.py:21
  43.3 38.7 %collective-permute-start.8 = (f16[512,1280]{1,0:T(8,128)(2,1)}, f16[512,1280]{1,0:T(8,128)(2,1)}, u32[]{:S(2)}, u32[]{:S(2)}) collective-permute-start(f16[512,1280]{1,0:T(8,128)(2,1)} %convert_element_type.126), channel_id=1, source_target_pairs={{0,2},{1,3},{2,0},{3,1},{4,6},{5,7},{6,4},{7,5},{8,10},{9,11},{10,... | collective-permute-start | bytes 3932168 | tf_op jit(solution)/shard_map/ppermute | solution.py:21
  45.0 7.3 %copy-start.17 = (f16[512,1280]{1,0:T(8,128)(2,1)S(1)}, f16[512,1280]{1,0:T(8,128)(2,1)}, u32[]{:S(2)}) copy-start(f16[512,1280]{1,0:T(8,128)(2,1)} %convert_element_type.125) | copy-start | bytes 3932164
  45.0 7.9 %copy-start = (bf16[512,3584]{1,0:T(8,128)(2,1)S(1)}, bf16[512,3584]{1,0:T(8,128)(2,1)}, u32[]{:S(2)}) copy-start(bf16[512,3584]{1,0:T(8,128)(2,1)} %hidden_ref.6) | copy-start | bytes 11010052
  52.3 23.2 %collective-permute-start.5 = (f32[512,1280]{1,0:T(8,128)}, f32[512,1280]{1,0:T(8,128)}, u32[]{:S(2)}, u32[]{:S(2)}) collective-permute-start(f32[512,1280]{1,0:T(8,128)} %shard_map.89), channel_id=1, source_target_pairs={{0,1},{1,0},{2,3},{3,2},{4,5},{5,4},{6,7},{7,6},{8,9},{9,8},{10,11... | collective-permute-start | bytes 7864328 | tf_op jit(solution)/shard_map/ppermute | solution.py:21
  52.3 50.5 %collective-permute-start.6 = (f16[512,1280]{1,0:T(8,128)(2,1)S(1)}, f16[512,1280]{1,0:T(8,128)(2,1)}, u32[]{:S(2)}, u32[]{:S(2)}) collective-permute-start(f16[512,1280]{1,0:T(8,128)(2,1)S(1)} %copy-done.17), channel_id=1, source_target_pairs={{0,2},{1,3},{2,0},{3,1},{4,6},{5,7},{6,4},{7,5},{8,10},{9,11},{10,... | collective-permute-start | bytes 3932168 | tf_op jit(solution)/shard_map/ppermute | solution.py:21
  52.8 15.2 %collective-permute-start.2 = (s32[128,160]{0,1:T(8,128)}, s32[128,160]{0,1:T(8,128)}, u32[]{:S(2)}, u32[]{:S(2)}) collective-permute-start(s32[128,160]{0,1:T(8,128)} %get-tuple-element.88), channel_id=1, source_target_pairs={{0,1},{1,0},{2,3},{3,2},{4,5},{5,4},{6,7},{7,6},{8,9},{9,8},{10,11... | collective-permute-start | bytes 245768 | tf_op jit(solution)/shard_map/ppermute | solution.py:192
  83.6 25.3 %copy-start.6 = (f32[512,1280]{1,0:T(8,128)}, f32[512,1280]{1,0:T(8,128)S(1)}, u32[]{:S(2)}) copy-start(f32[512,1280]{1,0:T(8,128)S(1)} %convert_add_fusion) | copy-start | bytes 7864324
  83.6 21.0 %copy-start.22 = (s32[512]{0:T(512)S(1)}, s32[512]{0:T(512)}, u32[]{:S(2)}) copy-start(s32[512]{0:T(512)} %param.11) | copy-start | bytes 6148
  102.8 6.1 %slice-start = ((s8[5242880]{0:T(1024)(128)(4,1)}), s8[4194304]{0:T(1024)(128)(4,1)S(1)}, s32[]{:S(2)}) async-start(s8[5242880]{0:T(1024)(128)(4,1)} %bitcast.86), calls=%async_computation | async-start | bytes 8388608
  104.6 4.3 %copy-start.7 = (f32[512,1280]{1,0:T(8,128)}, f32[512,1280]{1,0:T(8,128)S(1)}, u32[]{:S(2)}) copy-start(f32[512,1280]{1,0:T(8,128)S(1)} %convert_add_fusion.1) | copy-start | bytes 7864324
  104.6 4.3 %slice-start.1 = ((s8[5242880]{0:T(1024)(128)(4,1)}), s8[1048576]{0:T(1024)(128)(4,1)S(1)}, s32[]{:S(2)}) async-start(s8[5242880]{0:T(1024)(128)(4,1)} %bitcast.86), calls=%async_computation.1 | async-start | bytes 2097152
  108.9 4.9 %copy-start.14 = (pred[512,2560]{1,0:T(8,128)(4,1)}, pred[512,2560]{1,0:T(8,128)(4,1)S(1)}, u32[]{:S(2)}) copy-start(pred[512,2560]{1,0:T(8,128)(4,1)S(1)} %get-tuple-element.96) | copy-start | bytes 3932164
  155.9 8.7 %collective-permute-start.9 = (f16[2,2,2,2,16,1792]{5,4,0,1,2,3:T(8,128)(2,1)S(1)}, f16[2,2,2,2,16,1792]{5,4,0,1,2,3:T(8,128)(2,1)}, u32[]{:S(2)}, u32[]{:S(2)}) collective-permute-start(f16[2,2,2,2,16,1792]{5,4,0,1,2,3:T(8,128)(2,1)S(1)} %fusion.16), channel_id=1, source_target_pairs={{0,1},{1,0},{2,3},{3,2},{4,5},{5,4},{6,7},{7,6},{8,9},{9,8},{10,11... | collective-permute-start | bytes 2752520 | tf_op jit(solution)/shard_map/ppermute | solution.py:21
  155.9 8.7 %collective-permute-start.10 = (f16[2,2,2,2,16,1792]{5,4,0,1,3,2:T(8,128)(2,1)}, f16[2,2,2,2,16,1792]{5,4,0,1,3,2:T(8,128)(2,1)}, u32[]{:S(2)}, u32[]{:S(2)}) collective-permute-start(f16[2,2,2,2,16,1792]{5,4,0,1,3,2:T(8,128)(2,1)} %fusion.17), channel_id=1, source_target_pairs={{0,1},{1,0},{2,3},{3,2},{4,5},{5,4},{6,7},{7,6},{8,9},{9,8},{10,11... | collective-permute-start | bytes 2752520 | tf_op jit(solution)/shard_map/ppermute | solution.py:21
  156.4 2.0 copy-start.1
  161.5 3.1 %copy-start.12 = (f32[2,2,2,2,1,16,1792]{6,5,4,3,2,1,0:T(8,128)S(1)}, f32[2,2,2,2,1,16,1792]{6,5,4,3,2,1,0:T(8,128)}, u32[]{:S(2)}) copy-start(f32[2,2,2,2,1,16,1792]{6,5,4,3,2,1,0:T(8,128)} %get-tuple-element.78) | copy-start | bytes 5505028
  164.6 1.8 copy-start.13
  166.2 3.0 %copy-start.8 = (f32[2,2,2,2,16,1792]{5,4,0,1,2,3:T(8,128)}, f32[2,2,2,2,16,1792]{5,4,0,1,2,3:T(8,128)S(1)}, u32[]{:S(2)}) copy-start(f32[2,2,2,2,16,1792]{5,4,0,1,2,3:T(8,128)S(1)} %bitcast_add_fusion.1) | copy-start | bytes 5505028
  168.3 1.5 copy-start.10
  169.2 13.7 %collective-permute-start.11 = (f16[2,2,2,16,1792]{4,3,0,1,2:T(8,128)(2,1)S(1)}, f16[2,2,2,16,1792]{4,3,0,1,2:T(8,128)(2,1)S(1)}, u32[]{:S(2)}, u32[]{:S(2)}) collective-permute-start(f16[2,2,2,16,1792]{4,3,0,1,2:T(8,128)(2,1)S(1)} %fusion.18), channel_id=1, source_target_pairs={{0,2},{1,3},{2,0},{3,1},{4,6},{5,7},{6,4},{7,5},{8,10},{9,11},{10,... | collective-permute-start | bytes 1376264 | tf_op jit(solution)/shard_map/ppermute | solution.py:21
  169.8 13.8 %collective-permute-start.12 = (f16[2,2,2,16,1792]{4,3,0,1,2:T(8,128)(2,1)}, f16[2,2,2,16,1792]{4,3,0,1,2:T(8,128)(2,1)}, u32[]{:S(2)}, u32[]{:S(2)}) collective-permute-start(f16[2,2,2,16,1792]{4,3,0,1,2:T(8,128)(2,1)} %fusion.19), channel_id=1, source_target_pairs={{0,4},{4,0},{8,12},{12,8},{16,20},{20,16},{24,28},{28,24},{1,5},{5... | collective-permute-start | bytes 1376264 | tf_op jit(solution)/shard_map/ppermute | solution.py:21
  171.6 2.0 copy-start.2
  179.8 3.9 %copy-start.9 = (f32[2,2,2,2,16,1792]{5,4,0,1,2,3:T(8,128)S(1)}, f32[2,2,2,2,16,1792]{5,4,0,1,2,3:T(8,128)}, u32[]{:S(2)}) copy-start(f32[2,2,2,2,16,1792]{5,4,0,1,2,3:T(8,128)} %copy-done.8) | copy-start | bytes 5505028
  179.8 5.7 %copy-start.11 = (f32[2,2,2,2,16,1792]{5,4,0,1,3,2:T(8,128)S(1)}, f32[2,2,2,2,16,1792]{5,4,0,1,3,2:T(8,128)}, u32[]{:S(2)}) copy-start(f32[2,2,2,2,16,1792]{5,4,0,1,3,2:T(8,128)} %copy-done.10) | copy-start | bytes 5505028
  182.9 0.8 copy-start.18
  186.6 0.9 copy-start.15
  188.3 7.5 %collective-permute-start.13 = (f16[2,2,16,1792]{3,2,0,1:T(8,128)(2,1)}, f16[2,2,16,1792]{3,2,0,1:T(8,128)(2,1)}, u32[]{:S(2)}, u32[]{:S(2)}) collective-permute-start(f16[2,2,16,1792]{3,2,0,1:T(8,128)(2,1)} %fusion.23), channel_id=1, source_target_pairs={{0,4},{4,0},{8,12},{12,8},{16,20},{20,16},{24,28},{28,24},{1,5},{5... | collective-permute-start | bytes 688136 | tf_op jit(solution)/shard_map/ppermute | solution.py:21
  188.9 6.9 %collective-permute-start.14 = (f16[2,2,16,1792]{3,2,0,1:T(8,128)(2,1)}, f16[2,2,16,1792]{3,2,0,1:T(8,128)(2,1)}, u32[]{:S(2)}, u32[]{:S(2)}) collective-permute-start(f16[2,2,16,1792]{3,2,0,1:T(8,128)(2,1)} %fusion.24), channel_id=1, source_target_pairs={{0,2},{1,3},{2,0},{3,1},{4,6},{5,7},{6,4},{7,5},{8,10},{9,11},{10,... | collective-permute-start | bytes 688136 | tf_op jit(solution)/shard_map/ppermute | solution.py:21
  190.1 2.0 copy-start.3
  192.2 4.6 %copy-start.16 = (f32[2,2,2,16,1792]{4,3,0,1,2:T(8,128)S(1)}, f32[2,2,2,16,1792]{4,3,0,1,2:T(8,128)}, u32[]{:S(2)}) copy-start(f32[2,2,2,16,1792]{4,3,0,1,2:T(8,128)} %copy-done.15) | copy-start | bytes 2752516
  197.8 8.9 %copy-start.20 = (f32[1,512]{1,0:T(1,128)S(1)}, f32[1,512]{1,0:T(1,128)}, u32[]{:S(2)}) copy-start(f32[1,512]{1,0:T(1,128)} %get-tuple-element.89) | copy-start | bytes 6148
  197.8 8.9 %copy-start.21 = (f32[1,512]{1,0:T(1,128)S(1)}, f32[1,512]{1,0:T(1,128)}, u32[]{:S(2)}) copy-start(f32[1,512]{1,0:T(1,128)} %get-tuple-element.92) | copy-start | bytes 6148
  197.9 5.2 %collective-permute-start.15 = (f16[2,16,1792]{2,1,0:T(8,128)(2,1)S(1)}, f16[2,16,1792]{2,1,0:T(8,128)(2,1)S(1)}, u32[]{:S(2)}, u32[]{:S(2)}) collective-permute-start(f16[2,16,1792]{2,1,0:T(8,128)(2,1)S(1)} %fusion.25), channel_id=1, source_target_pairs={{0,8},{4,12},{8,0},{12,4},{16,24},{20,28},{24,16},{28,20},{1,9},{5... | collective-permute-start | bytes 344072 | tf_op jit(solution)/shard_map/ppermute | solution.py:21
  199.2 5.0 %collective-permute-start.16 = (f16[2,16,1792]{2,1,0:T(8,128)(2,1)S(1)}, f16[2,16,1792]{2,1,0:T(8,128)(2,1)S(1)}, u32[]{:S(2)}, u32[]{:S(2)}) collective-permute-start(f16[2,16,1792]{2,1,0:T(8,128)(2,1)S(1)} %fusion.26), channel_id=1, source_target_pairs={{0,8},{4,12},{8,0},{12,4},{16,24},{20,28},{24,16},{28,20},{1,9},{5... | collective-permute-start | bytes 344072 | tf_op jit(solution)/shard_map/ppermute | solution.py:21
  204.4 5.3 %collective-permute-start.18 = (f16[16,1792]{1,0:T(8,128)(2,1)S(1)}, f16[16,1792]{1,0:T(8,128)(2,1)S(1)}, u32[]{:S(2)}, u32[]{:S(2)}) collective-permute-start(f16[16,1792]{1,0:T(8,128)(2,1)S(1)} %fusion.28), channel_id=1, source_target_pairs={{0,16},{4,20},{8,24},{12,28},{16,0},{20,4},{24,8},{28,12},{1,17},{... | collective-permute-start | bytes 172040 | tf_op jit(solution)/shard_map/ppermute | solution.py:21
  208.0 5.1 %collective-permute-start.17 = (f16[16,1792]{1,0:T(8,128)(2,1)S(1)}, f16[16,1792]{1,0:T(8,128)(2,1)S(1)}, u32[]{:S(2)}, u32[]{:S(2)}) collective-permute-start(f16[16,1792]{1,0:T(8,128)(2,1)S(1)} %fusion.27), channel_id=1, source_target_pairs={{0,16},{4,20},{8,24},{12,28},{16,0},{20,4},{24,8},{28,12},{1,17},{... | collective-permute-start | bytes 172040 | tf_op jit(solution)/shard_map/ppermute | solution.py:21
